TPU v7x, 32 devices: a whole 2x2x4 slice. The times are simulated.
32 devices in a mesh: req: 16 (over z, y, x), blk: 2 (over core).
Axes of the slice: x: 2, y: 2, z: 4, core: 2. Of those that a mesh axis runs over, the one named last changes fastest.
Arguments:
- normed: bfloat16 [8192, 1536], P('req', 'blk'), may hold values from -6 to 6
- router: bfloat16 [1536, 16], P('blk'), may hold values from -0.15625 to 0.15625
- adapter_down: bfloat16 [1536, 256], P('blk'), may hold values from -0.15625 to 0.15625
- adapter_up: bfloat16 [256, 1536], P(None, 'blk'), may hold values from -1.5 to 1.5
- shared_gate_up: bfloat16 [1536, 2, 1024], P(None, None, 'blk'), may hold values from -0.15625 to 0.15625
- shared_down: bfloat16 [1024, 1536], P('blk'), may hold values from -0.1875 to 0.1875
- expert_gate_up: bfloat16 [16, 1536, 1024], P('req', 'blk'), may hold values from -0.15625 to 0.15625
- expert_down: bfloat16 [16, 512, 1536], P('req', None, 'blk'), may hold values from -0.25 to 0.25
- lengths: int32 [16, 4], P('req'), may hold values from 1 to 256, 512 in all within a row
- adapter_ids: int32 [16, 4], P('req'), may hold values from 0 to 15
- routes: int32 [8192, 6], P('req'), may hold values from 0 to 15, all different within a row; in each aligned block of 512 rows (0 to 511, 512 to 1023, ...) at most 208 rows name the same one
Outputs:
- mixed: bfloat16 [8192, 1536], P('req', 'blk')
Inputs may be any that keep to these rules, and one draw needn't show every extreme that they name: `lengths`: each row of an index of req lists its 4 prompts in token order; they sum to 512, the longest is 256. `routes`: each row names 6 different experts. Among the 512 rows of one index of req no expert is named more than 208 times, a bound that some block reaches.
All inputs are finite; a program needn't handle non-finite values.
Results may differ from a plain program's by a relative error of at most 0.013.
Values may be sent and summed in bfloat16 or wider, within the bound.
A program may use at most 128 MiB of HBM per device.

v0:
```python
import jax
import jax.numpy as jnp
from jax import lax
from jax.sharding import PartitionSpec as P

RANK = 16


def slot_table(target, source_row, total_slots):
    source_slot = jnp.zeros((total_slots,), jnp.int32).at[target].set(source_row)
    filled = jnp.zeros((total_slots,), jnp.int32).at[target].set(1)
    return (source_slot, filled)


def body(
    normed,
    router,
    adapter_down,
    adapter_up,
    shared_gate_up,
    shared_down,
    expert_gate_up,
    expert_down,
    lengths,
    adapter_ids,
    routes,
):
    tok_rows = normed.shape[0]
    feat_local = normed.shape[1]
    top_count = routes.shape[1]
    req_count = lax.axis_size("req")
    expert_count = req_count * expert_gate_up.shape[0]
    most_rows = (
        tok_rows * top_count + expert_count - 1
    ) // expert_count + tok_rows * top_count // (12 * expert_count)
    slot_count = req_count * most_rows
    hidden_width = expert_down.shape[1]
    logit_part = jnp.dot(normed, router, preferred_element_type=jnp.float32)
    low_part = jnp.dot(normed, adapter_down, preferred_element_type=jnp.float32)
    logits, low_all = (
        lax.psum(logit_part.astype(jnp.bfloat16), "blk").astype(jnp.float32),
        lax.psum(low_part.astype(jnp.bfloat16), "blk").astype(jnp.float32),
    )
    ends = jnp.cumsum(lengths[0])
    position = jnp.arange(tok_rows, dtype=jnp.int32)
    request = jnp.sum((position[:, None] >= ends[None, :]).astype(jnp.int32), axis=1)
    slots_req = jnp.arange(lengths.shape[1], dtype=jnp.int32)
    adapter_token = jnp.sum(
        jnp.where(request[:, None] == slots_req[None, :], adapter_ids[0][None, :], 0), axis=1
    )
    column_owner = jnp.arange(low_all.shape[1], dtype=jnp.int32) // RANK
    low = jnp.where(column_owner[None, :] == adapter_token[:, None], low_all, 0.0).astype(
        jnp.bfloat16
    )
    delta = jnp.dot(low, adapter_up, preferred_element_type=jnp.float32)
    shared_local = shared_gate_up.shape[2]
    shared_flat = shared_gate_up.reshape(shared_gate_up.shape[0], 2 * shared_local)
    shared_pre = jnp.dot(
        lax.all_gather(normed, "blk", axis=1, tiled=True),
        shared_flat,
        preferred_element_type=jnp.float32,
    )
    shared_hidden = (
        jax.nn.silu(shared_pre[:, :shared_local]) * shared_pre[:, shared_local:]
    ).astype(jnp.bfloat16)
    shared_terms = jnp.dot(shared_hidden, shared_down, preferred_element_type=jnp.float32)
    shared_out = lax.psum_scatter(
        shared_terms.astype(jnp.bfloat16), "blk", scatter_dimension=1, tiled=True
    ).astype(jnp.float32)
    scores = jax.nn.sigmoid(logits)
    chosen = jnp.take_along_axis(scores, routes, axis=1)
    gate_weight = chosen / jnp.sum(chosen, axis=1, keepdims=True)
    flat_expert = routes.reshape(-1)
    one_hot = (flat_expert[:, None] == jnp.arange(expert_count, dtype=jnp.int32)[None, :]).astype(
        jnp.int32
    )
    earlier = jnp.cumsum(one_hot, axis=0) - one_hot
    slot_rank = jnp.sum(earlier * one_hot, axis=1)
    source_row = jnp.arange(tok_rows * top_count, dtype=jnp.int32) // top_count
    weight_gate_up = expert_gate_up[0]
    weight_down = expert_down[0]
    target = flat_expert * most_rows + slot_rank
    source_slot, filled = slot_table(target, source_row, expert_count * most_rows)
    send_rows = jnp.where(filled[:, None] > 0, normed[source_slot], jnp.zeros((), jnp.bfloat16))
    received = lax.all_to_all(
        send_rows.reshape(expert_count, most_rows, feat_local),
        "req",
        split_axis=0,
        concat_axis=0,
        tiled=True,
    )
    rows_in = received.reshape(slot_count, feat_local)
    gate_up = lax.psum_scatter(
        jnp.dot(rows_in, weight_gate_up, preferred_element_type=jnp.float32).astype(jnp.bfloat16),
        "blk",
        scatter_dimension=0,
        tiled=True,
    ).astype(jnp.float32)
    hidden = (jax.nn.silu(gate_up[:, :hidden_width]) * gate_up[:, hidden_width:]).astype(
        jnp.bfloat16
    )
    expert_out = jnp.dot(
        lax.all_gather(hidden, "blk", axis=0, tiled=True),
        weight_down,
        preferred_element_type=jnp.float32,
    ).astype(jnp.bfloat16)
    returned = lax.all_to_all(
        expert_out.reshape(req_count, most_rows, feat_local),
        "req",
        split_axis=0,
        concat_axis=0,
        tiled=True,
    )
    picked = returned.reshape(expert_count * most_rows, feat_local)[target].astype(jnp.float32)
    weighted = picked * gate_weight.reshape(-1)[:, None]
    routed = jnp.sum(weighted.reshape(tok_rows, top_count, feat_local), axis=1)
    return (shared_out + 0.5 * delta + routed).astype(jnp.bfloat16)


def solution(mesh):
    return jax.shard_map(
        body,
        mesh=mesh,
        in_specs=(
            P("req", "blk"),
            P("blk", None),
            P("blk", None),
            P(None, "blk"),
            P(None, None, "blk"),
            P("blk", None),
            P("req", "blk", None),
            P("req", None, "blk"),
            P("req", None),
            P("req", None),
            P("req", None),
        ),
        out_specs=P("req", "blk"),
        check_vma=False,
    )
```

profile of v0, /device:TPU:14, one launch (start us, length us, event | category | flops | bytes accessed | tf_op | source)
XLA Modules:
  0.0 397.1 jit_solution(790846124738919260)
XLA Ops:
  6.5 1.0 copy.30
  7.6 0.2 eq.61
  7.7 0.2 eq.57
  7.9 0.7 broadcast_multiply_fusion
  8.6 4.6 %reduce-window.19 = s32[16,24,128]{2,1,0:T(8,128)S(1)} reduce-window(s32[16,24,128]{2,1,0:T(8,128)S(1)} %fusion.12, s32[]{:T(128)} %constant.58.clone.1), window={size=1x1x128 pad=0_0x0_0x127_0}, to_apply=%region_5.6 | reduce-window | flops 6242304 | bytes 393220 | tf_op jit(solution)/shard_map/reduce-window.1
  13.2 0.4 slice_reduce_fusion
  13.7 0.2 reduce-window.20
  13.9 0.1 broadcast_add_fusion
  14.0 0.1 copy.29
  14.2 0.2 mul.54
  14.4 0.1 fusion.11
  14.5 11.8 %scatter_custom_fusion.1 = s32[3328]{0:T(1024)S(1)} fusion(s32[3072]{0:T(1024)S(1)} %bitcast.56, s32[3072]{0:T(1024)S(1)} %add_select_fusion, s32[]{:T(128)} %constant.58.clone.1), kind=kCustom, calls=%fused_computation.49 | custom fusion | bytes 13316 | tf_op jit(solution)/shard_map/scatter | solution.py:10
  26.3 11.8 %scatter_custom_fusion = s32[3328]{0:T(1024)S(1)} fusion(s32[3072]{0:T(1024)S(1)} %bitcast.57, s32[3072]{0:T(1024)S(1)} %broadcast.128, s32[]{:T(128)} %constant.58.clone.1), kind=kCustom, calls=%fused_computation.52 | custom fusion | bytes 13316 | tf_op jit(solution)/shard_map/scatter | solution.py:11
  38.1 0.1 broadcast_in_dim.59
  38.2 10.7 %gather_fusion = bf16[3328,768]{1,0:T(8,128)(2,1)} fusion(bf16[512,768]{1,0:T(8,128)(2,1)S(1)} %copy-done.2, s32[4096]{0:T(1024)S(1)} %pad_clamp_fusion), kind=kCustom, calls=%fused_computation | custom fusion | bytes 10236928 | tf_op jit(solution)/shard_map/gather | solution.py:84
  49.0 3.5 broadcast_select_fusion
  52.4 118.3 %all_to_all.10 = bf16[16,208,768]{2,1,0:T(8,128)(2,1)S(1)} all-to-all(bf16[16,208,768]{2,1,0:T(8,128)(2,1)S(1)} %broadcast_select_fusion), channel_id=1, replica_groups=mesh['req'=16,'blk'=2] {'req'}, dimensions={0} | all-to-all | bytes 10223616 | tf_op jit(solution)/shard_map/all_to_all | solution.py:85
  170.7 7.5 %convolution_convert_fusion = bf16[3328,1024]{1,0:T(8,128)(2,1)} fusion(bf16[3328,768]{1,0:T(8,128)(2,1)S(1)} %bitcast.51, bf16[1,768,1024]{2,1,0:T(8,128)(2,1)S(1)} %copy-done), kind=kOutput, calls=%fused_computation.6 | convolution fusion | flops 5237899264 | bytes 13500416 | tf_op jit(solution)/shard_map/dot_general | solution.py:94
  178.2 0.0 all-gather.5.cloned.1.call-start
  178.3 15.4 %reduce-scatter.5.cloned.1.call-done = bf16[1664,1024]{1,0:T(8,128)(2,1)} async-done(((bf16[3328,1024]{1,0:T(8,128)(2,1)}), bf16[1664,1024]{1,0:T(8,128)(2,1)}) %reduce-scatter.5.cloned.1.call-update) | async-done | bytes 3407888 | tf_op jit(solution)/shard_map/reduce_scatter | solution.py:93
  193.7 2.8 convert_element_type.66
  196.5 2.4 fusion
  198.9 13.9 %all-gather.5.cloned.1.call-done = bf16[3328,512]{1,0:T(8,128)(2,1)} async-done(((bf16[1664,512]{1,0:T(8,128)(2,1)}), bf16[3328,512]{1,0:T(8,128)(2,1)}) %all-gather.5.cloned.1.call-update) | async-done | bytes 3407888 | tf_op jit(solution)/shard_map/all_gather | solution.py:103
  212.8 7.1 %convolution_convert_fusion.1 = bf16[3328,768]{1,0:T(8,128)(2,1)} fusion(bf16[3328,512]{1,0:T(8,128)(2,1)} %all-gather.5.cloned.1.call-done, bf16[1,512,768]{2,1,0:T(8,128)(2,1)S(1)} %copy-done.9), kind=kOutput, calls=%fused_computation.7 | convolution fusion | flops 2619801600 | bytes 9306112 | tf_op jit(solution)/shard_map/dot_general | solution.py:102
  219.9 7.1 %all-to-all-start.1 = ((bf16[16,208,768]{2,1,0:T(8,128)(2,1)}), bf16[16,208,768]{2,1,0:T(8,128)(2,1)}, u32[]{:S(2)}, u32[]{:S(2)}) async-start(bf16[16,208,768]{2,1,0:T(8,128)(2,1)} %bitcast.50), calls=%async_computation.3 | async-start | bytes 10223616 | tf_op jit(solution)/shard_map/all_to_all | solution.py:107
  227.0 0.2 all-gather.3.cloned.1.call-start
  227.2 0.5 all-gather.3.cloned.1.call-update
  227.8 1.1 convolution_convert_fusion.3
  229.0 4.5 %copy.35 = bf16[192,8,2,512]{3,1,2,0:T(8,128)(2,1)} copy(bf16[192,8,2,512]{3,2,1,0:T(2,128)(2,1)} %bitcast.52) | data formatting | bytes 6291456
  233.4 7.0 %all-gather.3.cloned.1.call-done = bf16[512,1536]{1,0:T(8,128)(2,1)} async-done(((bf16[512,768]{1,0:T(8,128)(2,1)}), bf16[512,1536]{1,0:T(8,128)(2,1)}) %all-gather.3.cloned.1.call-update) | async-done | bytes 1572880 | tf_op jit(solution)/shard_map/all_gather | solution.py:59
  240.4 4.3 %fusion.23 = f32[512,1024]{1,0:T(8,128)S(1)} fusion(bf16[512,1536]{1,0:T(8,128)(2,1)} %all-gather.3.cloned.1.call-done, bf16[1536,1024]{1,0:T(8,128)(2,1)} %bitcast.53), kind=kOutput, calls=%fused_computation.66 | convolution fusion | flops 1610612736 | bytes 6815744 | tf_op jit(solution)/shard_map/dot_general | solution.py:58
  244.7 2.2 convolution_convert_fusion.2
  247.0 0.1 copy.32
  247.2 0.2 reshape.164
  247.3 0.3 convolution_convert_fusion.4
  247.6 3.5 psum.15
  251.2 24.9 %gather_fusion.2 = f32[3072]{0:T(1024)S(1)} fusion(f32[512,16]{0,1:T(8,128)S(1)} %add_divide_fusion, s32[3072]{0:T(1024)S(1)} %reshape.164), kind=kCustom, calls=%fused_computation.2 | custom fusion | bytes 49152 | tf_op jit(solution)/shard_map/jit(take_along_axis)/gather | solution.py:71
  276.1 0.2 reshape.167
  276.3 0.1 copy.33
  276.5 0.1 copy.34
  276.7 0.2 reduce-window.18
  276.9 0.1 convert_reduce_fusion
  276.9 0.1 select_reduce_fusion
  277.0 66.7 %all-to-all-done.1 = bf16[16,208,768]{2,1,0:T(8,128)(2,1)} async-done(((bf16[16,208,768]{2,1,0:T(8,128)(2,1)}), bf16[16,208,768]{2,1,0:T(8,128)(2,1)}, u32[]{:S(2)}, u32[]{:S(2)}) %all-to-all-start.1) | async-done | bytes 5111840 | tf_op jit(solution)/shard_map/all_to_all | solution.py:107
  343.8 17.7 %gather_fusion.1 = bf16[3072,768]{1,0:T(8,128)(2,1)} fusion(bf16[3328,768]{1,0:T(8,128)(2,1)} %bitcast.11, s32[3072]{0:T(1024)S(1)} %broadcast_clamp_fusion), kind=kCustom, calls=%fused_computation.1 | custom fusion | bytes 9449472 | tf_op jit(solution)/shard_map/gather | solution.py:114
  361.4 9.2 %reshape.147 = f32[512,6,768]{2,1,0:T(8,128)} reshape(bf16[3072,768]{1,0:T(8,128)(2,1)} %gather_fusion.1) | data formatting | bytes 14155776 | tf_op jit(solution)/shard_map/convert_element_type | solution.py:114
  370.6 17.2 %multiply_reduce_fusion = f32[512,768]{1,0:T(8,128)S(1)} fusion(f32[512,6,768]{2,1,0:T(8,128)} %reshape.147, f32[512,6]{1,0:T(8,128)S(1)} %copy.34), kind=kLoop, calls=%fused_computation.5 | loop fusion | flops 4325376 | bytes 11022336 | tf_op jit(solution)/shard_map/reduce_sum | solution.py:116
  387.9 2.7 add_convert_fusion
  (44 shorter events, 0.4 us)
Async XLA Ops:
  6.5 164.2 %copy-start = (bf16[1,768,1024]{2,1,0:T(8,128)(2,1)S(1)}, bf16[1,768,1024]{2,1,0:T(8,128)(2,1)}, u32[]{:S(2)}) copy-start(bf16[1,768,1024]{2,1,0:T(8,128)(2,1)} %param.17) | copy-start | bytes 4718596
  6.5 31.7 %copy-start.2 = (bf16[512,768]{1,0:T(8,128)(2,1)S(1)}, bf16[512,768]{1,0:T(8,128)(2,1)}, u32[]{:S(2)}) copy-start(bf16[512,768]{1,0:T(8,128)(2,1)} %param.11) | copy-start | bytes 2359300
  6.5 187.2 %reduce-scatter.5.cloned.1.call-start = ((), (), s32[]{:S(2)}) async-start(), calls=%async_computation.7 | async-start | bytes 10223616 | tf_op jit(solution)/shard_map/reduce_scatter | solution.py:93
  178.2 34.6 %all-gather.5.cloned.1.call-start = ((), (), s32[]{:S(2)}) async-start(), calls=%async_computation.8 | async-start | bytes 5111808 | tf_op jit(solution)/shard_map/all_gather | solution.py:103
  196.5 16.3 %copy-start.9 = (bf16[1,512,768]{2,1,0:T(8,128)(2,1)S(1)}, bf16[1,512,768]{2,1,0:T(8,128)(2,1)}, u32[]{:S(2)}) copy-start(bf16[1,512,768]{2,1,0:T(8,128)(2,1)} %param.18) | copy-start | bytes 2359300
  219.9 7.9 %copy-start.3 = (bf16[512,768]{1,0:T(8,128)(2,1)S(1)}, bf16[512,768]{1,0:T(8,128)(2,1)}, u32[]{:S(2)}) copy-start(bf16[512,768]{1,0:T(8,128)(2,1)} %param.11) | copy-start | bytes 2359300
  219.9 7.9 %copy-start.5 = (bf16[768,256]{1,0:T(8,128)(2,1)S(1)}, bf16[768,256]{1,0:T(8,128)(2,1)}, u32[]{:S(2)}) copy-start(bf16[768,256]{1,0:T(8,128)(2,1)} %param.13) | copy-start | bytes 1179652
  219.9 123.8 %all-to-all-start.1 = ((bf16[16,208,768]{2,1,0:T(8,128)(2,1)}), bf16[16,208,768]{2,1,0:T(8,128)(2,1)}, u32[]{:S(2)}, u32[]{:S(2)}) async-start(bf16[16,208,768]{2,1,0:T(8,128)(2,1)} %bitcast.50), calls=%async_computation.3 | async-start | bytes 10223616 | tf_op jit(solution)/shard_map/all_to_all | solution.py:107
  227.0 13.4 %all-gather.3.cloned.1.call-start = ((), (), s32[]{:S(2)}) async-start(), calls=%async_computation.4 | async-start | bytes 2359296 | tf_op jit(solution)/shard_map/all_gather | solution.py:59
  227.7 160.1 %all-reduce.2.cloned.1.call-start = ((), (), s32[]{:S(2)}) async-start(), calls=%async_computation.6 | async-start | bytes 524288 | tf_op jit(solution)/shard_map/psum | solution.py:42
  228.9 158.9 %reduce-scatter.3.cloned.1.call-start = ((), (), s32[]{:S(2)}) async-start(), calls=%async_computation.5 | async-start | bytes 2359296 | tf_op jit(solution)/shard_map/reduce_scatter | solution.py:67
  240.4 4.3 %copy-start.8 = (bf16[512,1536]{1,0:T(8,128)(2,1)S(1)}, bf16[512,1536]{1,0:T(8,128)(2,1)}, u32[]{:S(2)}) copy-start(bf16[512,1536]{1,0:T(8,128)(2,1)} %param.16) | copy-start | bytes 4718596
  244.7 2.3 copy-start.4
  244.7 2.6 copy-start.6
  251.2 25.5 %copy-start.10 = (s32[1,4]{1,0:T(1,128)S(1)}, s32[1,4]{1,0:T(1,128)}, u32[]{:S(2)}) copy-start(s32[1,4]{1,0:T(1,128)} %param.19) | copy-start | bytes 52
  251.2 25.7 %copy-start.7 = (s32[1,4]{1,0:T(1,128)S(1)}, s32[1,4]{1,0:T(1,128)}, u32[]{:S(2)}) copy-start(s32[1,4]{1,0:T(1,128)} %param.20) | copy-start | bytes 52
  370.6 19.9 %copy-start.1 = (bf16[1,768,1024]{2,1,0:T(8,128)(2,1)S(1)}, bf16[1,768,1024]{2,1,0:T(8,128)(2,1)}, u32[]{:S(2)}) copy-start(bf16[1,768,1024]{2,1,0:T(8,128)(2,1)} %param.17) | copy-start | bytes 4718596
Sparse Core Ops, SparseCore 0:
  178.4 15.3 reduce-scatter.4
  199.1 13.7 all-gather.4
  229.5 10.9 all-gather.2
  242.7 19.4 all-reduce.1
  264.3 10.2 reduce-scatter.2
where the time goes:
time: 398 us; the launch traced here: 397 us
  blocking collectives  122 us (31%)
  waiting for transfers between devices  104 us (26%)
  local copies, waits for them, and re-layouts  93.6 us (24%)
  other arithmetic  32 us (8%)
  matrix products  25.1 us (6%)
  between operations  13.5 us (3%)
  starting transfers between devices  7.43 us (2%)
    all_to_all x1, blocking collectives, body(): lax.all_to_all(send_rows.reshape(expert_count, most_rows, feat_local), 'r...  118 us
    all_to_all x1, waiting for transfers between devices, body(): lax.all_to_all(expert_out.reshape(req_count, most_rows, feat_local), 'req...  66.7 us
    gather x5, local copies, waits for them, and re-layouts, body(): chosen = jnp.take_along_axis(scores, routes, axis=1)  25.5 us
    gather x1, local copies, waits for them, and re-layouts, body(): returned.reshape(expert_count * most_rows, feat_local)[target]  17.7 us
    reduce_sum x1, other arithmetic, body(): routed = jnp.sum(weighted.reshape(tok_rows, top_count, feat_local), axis=1)  17.2 us
    reduce_scatter x1, waiting for transfers between devices, body(): lax.psum_scatter(jnp.dot(rows_in, weight_gate_up, preferred_element_type=...  15.4 us
    all_gather x1, waiting for transfers between devices, body(): lax.all_gather(hidden, 'blk', axis=0, tiled=True)  13.9 us
    scatter x1, local copies, waits for them, and re-layouts, slot_table(): filled = jnp.zeros((total_slots,), jnp.int32).at[target].set(1)  11.8 us
  transfers between devices with their start and end apart: 6, of which 4 were waited for; matrix products, arithmetic and copies ran while one was open for 21% of the time, Pallas kernels for 0%

commit v1 on v0

v1 whole, which is shorter than its diff:
```python
import jax
import jax.numpy as jnp
from jax import lax
from jax.sharding import PartitionSpec as P

RANK = 16
DEPTH = 4


def body(
    normed,
    router,
    adapter_down,
    adapter_up,
    shared_gate_up,
    shared_down,
    expert_gate_up,
    expert_down,
    lengths,
    adapter_ids,
    routes,
):
    f32, bf16 = jnp.float32, jnp.bfloat16
    tok_rows, feat_local = normed.shape
    feat = 2 * feat_local
    req_count = lax.axis_size("req")
    expert_count = req_count
    plane = req_count // DEPTH
    hidden_width = expert_down.shape[1]
    half = hidden_width // 2
    planes = [[z * plane + p for p in range(plane)] for z in range(DEPTH)]
    columns = [[z * plane + p for z in range(DEPTH)] for p in range(plane)]
    my_z = lax.axis_index("req") // plane

    gu = expert_gate_up[0].reshape(feat_local, 2, 2, half).transpose(2, 0, 1, 3)
    gu = gu.reshape(2 * feat_local, 2 * half)
    gu = lax.all_to_all(gu, "blk", split_axis=0, concat_axis=0, tiled=True)
    down = lax.all_to_all(expert_down[0], "blk", split_axis=0, concat_axis=1, tiled=True)
    gu_all = lax.all_gather(gu, "req", axis_index_groups=planes)
    down_all = lax.all_gather(down, "req", axis_index_groups=planes)

    x_half = lax.all_gather(normed, "req", axis_index_groups=columns, tiled=True)
    x_own = lax.all_gather(normed, "blk", axis=1, tiled=True)
    x_all = lax.all_gather(x_half, "blk", axis=1, tiled=True)

    router_full = lax.all_gather(router, "blk", axis=0, tiled=True)
    logits = jnp.dot(x_own, router_full, preferred_element_type=f32)
    scores = jax.nn.sigmoid(logits)
    experts = jnp.arange(expert_count, dtype=jnp.int32)
    named = jnp.zeros((tok_rows, expert_count), jnp.bool_)
    for k in range(routes.shape[1]):
        named = named | (routes[:, k : k + 1] == experts[None, :])
    chosen = jnp.where(named, scores, 0.0)
    gate = chosen / jnp.sum(chosen, axis=1, keepdims=True)
    gate_all = lax.all_gather(gate, "req", axis_index_groups=columns, tiled=True)
    gate_here = lax.dynamic_slice_in_dim(gate_all, my_z * plane, plane, axis=1)

    low_part = jnp.dot(normed, adapter_down, preferred_element_type=f32)
    low_all = lax.psum(low_part.astype(bf16), "blk").astype(f32)
    ends = jnp.cumsum(lengths[0])
    position = jnp.arange(tok_rows, dtype=jnp.int32)
    request = jnp.sum((position[:, None] >= ends[None, :]).astype(jnp.int32), axis=1)
    slots_req = jnp.arange(lengths.shape[1], dtype=jnp.int32)
    adapter_token = jnp.sum(
        jnp.where(request[:, None] == slots_req[None, :], adapter_ids[0][None, :], 0), axis=1
    )
    column_owner = jnp.arange(low_all.shape[1], dtype=jnp.int32) // RANK
    low = jnp.where(column_owner[None, :] == adapter_token[:, None], low_all, 0.0).astype(bf16)
    delta = jnp.dot(low, adapter_up, preferred_element_type=f32)

    shared_gate = jnp.dot(x_own, shared_gate_up[:, 0, :], preferred_element_type=f32)
    shared_up = jnp.dot(x_own, shared_gate_up[:, 1, :], preferred_element_type=f32)
    shared_hidden = (jax.nn.silu(shared_gate) * shared_up).astype(bf16)
    shared_terms = jnp.dot(shared_hidden, shared_down, preferred_element_type=f32)
    shared_out = lax.psum_scatter(
        shared_terms.astype(bf16), "blk", scatter_dimension=1, tiled=True
    ).astype(f32)

    pieces = []
    for p in range(plane):
        gate_p = jnp.dot(x_all, gu_all[p, :, :half], preferred_element_type=f32)
        up_p = jnp.dot(x_all, gu_all[p, :, half:], preferred_element_type=f32)
        pieces.append((jax.nn.silu(gate_p) * up_p * gate_here[:, p : p + 1]).astype(bf16))
    hidden = jnp.concatenate(pieces, axis=1)
    terms = jnp.dot(hidden, down_all.reshape(plane * half, feat), preferred_element_type=f32)
    terms = lax.psum_scatter(terms.astype(bf16), "blk", scatter_dimension=1, tiled=True)
    routed = lax.psum_scatter(
        terms, "req", scatter_dimension=0, axis_index_groups=columns, tiled=True
    ).astype(f32)
    return (shared_out + 0.5 * delta + routed).astype(bf16)


def solution(mesh):
    return jax.shard_map(
        body,
        mesh=mesh,
        in_specs=(
            P("req", "blk"),
            P("blk", None),
            P("blk", None),
            P(None, "blk"),
            P(None, None, "blk"),
            P("blk", None),
            P("req", "blk", None),
            P("req", None, "blk"),
            P("req", None),
            P("req", None),
            P("req", None),
        ),
        out_specs=P("req", "blk"),
        check_vma=False,
    )
```

time: 398 us -> 357 us (0.90)
  waiting for transfers between devices: 104 us -> 253 us
  blocking collectives: 122 us -> 24.9 us
  local copies, waits for them, and re-layouts: 93.6 us -> 16.7 us
  other arithmetic: 32 us -> 0.36 us
  matrix products: 25.1 us -> 46.6 us
  starting transfers between devices: 7.43 us -> 0.33 us
    all_gather x2 -> x5, waiting for transfers between devices: 20.9 us -> 157 us  [the longest x1 56.4 us: body(): gu_all = lax.all_gather(gu, 'req', axis_index_groups=planes)]
    all_to_all x1 -> x2, blocking collectives: 118 us -> 9.36 us  [the longest x1 5 us: body(): gu = lax.all_to_all(gu, 'blk', split_axis=0, concat_axis=0, tiled=True)]
    all_to_all x1 -> x0, waiting for transfers between devices: 66.7 us -> none  [body(): lax.all_to_all(expert_out.reshape(req_count, most_rows, feat_local), 'req...]
    reduce_scatter x2 -> x3, waiting for transfers between devices: 15.5 us -> 75.7 us  [the longest x1 63.1 us: body(): lax.psum_scatter(terms, 'req', scatter_dimension=0, axis_index_groups=col...]
    gather x7 -> x0, local copies, waits for them, and re-layouts: 54 us -> none  [the longest x5 25.5 us: body(): chosen = jnp.take_along_axis(scores, routes, axis=1)]
    scatter x2 -> x0, local copies, waits for them, and re-layouts: 23.6 us -> none  [the longest x1 11.8 us: slot_table(): filled = jnp.zeros((total_slots,), jnp.int32).at[target].set(1)]
    dot_general x7 -> x14, matrix products: 25.1 us -> 46.6 us  [the longest x4 11.8 us: body(): up_p = jnp.dot(x_all, gu_all[p, :, half:], preferred_element_type=f32)]
    psum x1, waiting for transfers between devices: 0.02 us -> 17.8 us  [body(): low_all = lax.psum(low_part.astype(bf16), 'blk').astype(f32)]
  transfers between devices with their start and end apart: 6 -> 9, of which waited for: 4 -> 8; matrix products, arithmetic and copies ran while one was open for 21% -> 13% of each run, Pallas kernels for 0% -> 0%
where the time goes in v1:
time: 357 us; the launch traced here: 355 us
  waiting for transfers between devices  253 us (71%)
  matrix products  46.6 us (13%)
  blocking collectives  24.9 us (7%)
  local copies, waits for them, and re-layouts  16.7 us (5%)
  between operations  13.4 us (4%)
    reduce_scatter x1, waiting for transfers between devices, body(): lax.psum_scatter(terms, 'req', scatter_dimension=0, axis_index_groups=col...  63.1 us
    all_gather x1, waiting for transfers between devices, body(): gu_all = lax.all_gather(gu, 'req', axis_index_groups=planes)  56.4 us
    all_gather x1, waiting for transfers between devices, body(): lax.all_gather(normed, 'req', axis_index_groups=columns, tiled=True)  54.7 us
    all_gather x1, waiting for transfers between devices, body(): down_all = lax.all_gather(down, 'req', axis_index_groups=planes)  21.7 us
    all_gather x1, waiting for transfers between devices, body(): x_all = lax.all_gather(x_half, 'blk', axis=1, tiled=True)  19.4 us
    psum x1, waiting for transfers between devices, body(): low_all = lax.psum(low_part.astype(bf16), 'blk').astype(f32)  17.8 us
    all_gather x1, blocking collectives, body(): lax.all_gather(gate, 'req', axis_index_groups=columns, tiled=True)  13.7 us
    reduce_scatter x1, waiting for transfers between devices, body(): lax.psum_scatter(shared_terms.astype(bf16), 'blk', scatter_dimension=1, t...  12.5 us
  transfers between devices with their start and end apart: 9, of which 8 were waited for; matrix products, arithmetic and copies ran while one was open for 13% of the time, Pallas kernels for 0%

profile of v1, /device:TPU:14, one launch (start us, length us, event | category | flops | bytes accessed | tf_op | source)
XLA Modules:
  0.0 354.7 jit_solution(9512838211663802107)
XLA Ops:
  6.5 0.7 all-gather.8.cloned.1.call-update
  7.3 0.7 all-gather.6.cloned.1.call-update
  8.0 0.0 all-gather.12.cloned.1.call-start
  8.1 1.7 copy.30
  9.8 0.1 copy.31
  9.9 5.0 %all_to_all.25 = bf16[2,768,512]{1,2,0:T(8,128)(2,1)S(1)} all-to-all(bf16[2,768,512]{1,2,0:T(8,128)(2,1)S(1)} %bitcast.76), channel_id=1, replica_groups=mesh['req'=16,'blk'=2] {'blk'}, dimensions={0} | all-to-all | bytes 3145728 | tf_op jit(solution)/shard_map/all_to_all | solution.py:37
  14.9 1.6 copy.32
  16.5 0.0 all-gather.10.cloned.1.call-start
  16.5 54.7 %all-gather.8.cloned.1.call-done = bf16[2048,768]{1,0:T(8,128)(2,1)} async-done(((bf16[512,768]{1,0:T(8,128)(2,1)}), bf16[2048,768]{1,0:T(8,128)(2,1)}) %all-gather.8.cloned.1.call-update) | async-done | bytes 3145744 | tf_op jit(solution)/shard_map/all_gather | solution.py:42
  71.3 0.0 all-gather.14.cloned.1.call-start
  71.4 4.4 %all_to_all.26 = bf16[2,256,768]{2,1,0:T(8,128)(2,1)S(1)} all-to-all(bf16[2,256,768]{2,1,0:T(8,128)(2,1)S(1)} %bitcast.80), channel_id=1, replica_groups=mesh['req'=16,'blk'=2] {'blk'}, dimensions={0} | all-to-all | bytes 1572864 | tf_op jit(solution)/shard_map/all_to_all | solution.py:38
  75.7 0.3 copy.33
  76.0 1.2 copy.34
  77.2 0.0 reduce-scatter.6.cloned.1.call-start
  77.3 1.8 all_gather.32
  79.1 4.7 %all-gather.6.cloned.1.call-done = bf16[512,1536]{1,0:T(8,128)(2,1)} async-done(((bf16[512,768]{1,0:T(8,128)(2,1)}), bf16[512,1536]{1,0:T(8,128)(2,1)}) %all-gather.6.cloned.1.call-update) | async-done | bytes 1572880 | tf_op jit(solution)/shard_map/all_gather | solution.py:43
  83.8 2.0 fusion.41
  85.8 13.7 %all_gather.33 = f32[2048,16]{0,1:T(8,128)S(1)} all-gather(f32[512,16]{0,1:T(8,128)S(1)} %broadcast_divide_fusion), channel_id=1, replica_groups={{0,8,16,24},{2,10,18,26},{4,12,20,28},{6,14,22,30},{1,9,17,25},{3,11,19..., dimensions={0}, use_global_device_ids=true | all-gather | bytes 163840 | tf_op jit(solution)/shard_map/all_gather | solution.py:55
  99.5 56.4 %all-gather.12.cloned.1.call-done = bf16[4,1536,512]{2,1,0:T(8,128)(2,1)} async-done(((bf16[1,1536,512]{2,1,0:T(8,128)(2,1)}), bf16[4,1536,512]{2,1,0:T(8,128)(2,1)}) %all-gather.12.cloned.1.call-update) | async-done | bytes 6291472 | tf_op jit(solution)/shard_map/all_gather | solution.py:39
  155.9 19.4 %all-gather.10.cloned.1.call-done = bf16[2048,1536]{1,0:T(8,128)(2,1)} async-done(((bf16[2048,768]{1,0:T(8,128)(2,1)}), bf16[2048,1536]{1,0:T(8,128)(2,1)}) %all-gather.10.cloned.1.call-update) | async-done | bytes 6291472 | tf_op jit(solution)/shard_map/all_gather | solution.py:44
  175.3 4.9 %fusion.26 = f32[2048,256]{0,1:T(8,128)S(1)} fusion(bf16[2048,1536]{1,0:T(8,128)(2,1)} %all-gather.10.cloned.1.call-done, bf16[4,1536,512]{2,1,0:T(8,128)(2,1)} %all-gather.12.cloned.1.call-done), kind=kOutput, calls=%fused_computation.45 | convolution fusion | flops 1610612736 | bytes 9175040 | tf_op jit(solution)/shard_map/dot_general | solution.py:81
  180.2 1.7 copy-done.9
  181.9 1.9 fusion.25
  183.7 1.8 fusion.24
  185.6 1.8 fusion.23
  187.5 2.2 fusion.11
  189.6 3.1 fusion.12
  192.8 3.4 fusion.13
  196.1 3.1 fusion.14
  199.2 21.7 %all-gather.14.cloned.1.call-done = bf16[4,256,1536]{2,1,0:T(8,128)(2,1)} async-done(((bf16[1,256,1536]{2,1,0:T(8,128)(2,1)}), bf16[4,256,1536]{2,1,0:T(8,128)(2,1)}) %all-gather.14.cloned.1.call-update) | async-done | bytes 3145744 | tf_op jit(solution)/shard_map/all_gather | solution.py:40
  220.9 11.0 %convolution_convert_fusion = bf16[2048,1536]{1,0:T(8,128)(2,1)} fusion(bf16[1024,1536]{1,0:T(8,128)(2,1)} %bitcast.93, bf16[2048,256]{0,1:T(8,128)(2,1)} %fusion.14, bf16[2048,256]{0,1:T(8,128)(2,1)} %fusion.13, bf16[2048,256]{0,1:T(8,128)(2,1)} %fusion.12, bf16[2048,256]{0,1:T(8,128)(2,1)S(1)} %fusion.11), kind=kOutput, calls=%fused_computation | convolution fusion | flops 6462373888 | bytes 13631488 | tf_op jit(solution)/shard_map/dot_general | solution.py:85
  232.0 0.0 all-reduce.2.cloned.1.call-start
  232.1 1.1 copy-done.1
  233.1 0.1 copy-done.4
  233.2 1.1 convolution_convert_fusion.2
  234.3 0.0 reduce-scatter.4.cloned.1.call-start
  234.4 9.0 %fusion.39 = (bf16[1536,1,512]{2,1,0:T(2,128)(2,1)S(1)}, bf16[1536,1,512]{2,1,0:T(2,128)(2,1)}) fusion(bf16[1536,2,512]{2,1,0:T(2,128)(2,1)} %param.15), kind=kLoop, calls=%fused_computation.78 | loop fusion | bytes 6291456 | tf_op jit(solution)/shard_map/slice | solution.py:71
  243.4 1.9 fusion.16
  245.3 5.5 %convolution_convert_fusion.1 = bf16[512,1536]{1,0:T(8,128)(2,1)} fusion(bf16[512,1536]{1,0:T(8,128)(2,1)S(1)} %copy-done, bf16[512,1536]{1,0:T(8,128)(2,1)S(1)} %copy-done.2, bf16[1536,1,512]{2,1,0:T(2,128)(2,1)} %get-tuple-element.6, f32[512,512]{1,0:T(8,128)} %fusion.16), kind=kOutput, calls=%fused_computation.8 | convolution fusion | flops 1612972032 | bytes 7340032 | tf_op jit(solution)/shard_map/dot_general | solution.py:74
  250.8 0.0 reduce-scatter.8.cloned.1.call-start
  250.9 0.7 reduce-scatter.8.cloned.1.call-update
  251.6 0.2 reduce-window.8
  251.8 0.1 convert_reduce_fusion
  251.9 0.1 select_reduce_fusion
  251.9 17.8 %all-reduce.2.cloned.1.call-done = bf16[512,256]{1,0:T(8,128)(2,1)} async-done(((bf16[512,256]{1,0:T(8,128)(2,1)}), bf16[512,256]{1,0:T(8,128)(2,1)}) %all-reduce.2.cloned.1.call-update) | async-done | bytes 262160 | tf_op jit(solution)/shard_map/psum | solution.py:59
  269.7 12.5 %reduce-scatter.4.cloned.1.call-done = bf16[512,768]{1,0:T(8,128)(2,1)} async-done(((bf16[512,1536]{1,0:T(8,128)(2,1)}), bf16[512,768]{1,0:T(8,128)(2,1)}) %reduce-scatter.4.cloned.1.call-update) | async-done | bytes 786448 | tf_op jit(solution)/shard_map/reduce_scatter | solution.py:75
  282.3 63.1 %reduce-scatter.8.cloned.1.call-done = bf16[512,768]{1,0:T(8,128)(2,1)} async-done(((bf16[2048,768]{1,0:T(8,128)(2,1)}), bf16[512,768]{1,0:T(8,128)(2,1)}) %reduce-scatter.8.cloned.1.call-update) | async-done | bytes 786448 | tf_op jit(solution)/shard_map/reduce_scatter | solution.py:87
  345.4 2.8 add_convert_fusion
  (34 shorter events, 0.2 us)
Async XLA Ops:
  6.5 238.8 %copy-start = (bf16[512,1536]{1,0:T(8,128)(2,1)S(1)}, bf16[512,1536]{1,0:T(8,128)(2,1)}, u32[]{:S(2)}) copy-start(bf16[512,1536]{1,0:T(8,128)(2,1)} %param.16) | copy-start | bytes 4718596
  6.5 64.7 %all-gather.8.cloned.1.call-start = ((), (), s32[]{:S(2)}) async-start(), calls=%async_computation.8 | async-start | bytes 3932160 | tf_op jit(solution)/shard_map/all_gather | solution.py:42
  7.3 76.6 %all-gather.6.cloned.1.call-start = ((), (), s32[]{:S(2)}) async-start(), calls=%async_computation.5 | async-start | bytes 2359296 | tf_op jit(solution)/shard_map/all_gather | solution.py:43
  8.0 147.9 %all-gather.12.cloned.1.call-start = ((), (), s32[]{:S(2)}) async-start(), calls=%async_computation.10 | async-start | bytes 7864320 | tf_op jit(solution)/shard_map/all_gather | solution.py:39
  16.5 54.9 %copy-start.3 = (bf16[1,512,768]{2,1,0:T(8,128)(2,1)S(1)}, bf16[1,512,768]{2,1,0:T(8,128)(2,1)}, u32[]{:S(2)}) copy-start(bf16[1,512,768]{2,1,0:T(8,128)(2,1)} %param.18) | copy-start | bytes 2359300
  16.5 158.8 %all-gather.10.cloned.1.call-start = ((), (), s32[]{:S(2)}) async-start(), calls=%async_computation.9 | async-start | bytes 9437184 | tf_op jit(solution)/shard_map/all_gather | solution.py:44
  71.3 149.7 %all-gather.14.cloned.1.call-start = ((), (), s32[]{:S(2)}) async-start(), calls=%async_computation.11 | async-start | bytes 3932160 | tf_op jit(solution)/shard_map/all_gather | solution.py:40
  75.7 1.5 copy-start.6
  75.7 1.6 copy-start.5
  77.2 173.7 %reduce-scatter.6.cloned.1.call-start = ((), (), s32[]{:S(2)}) async-start(), calls=%async_computation.12 | async-start | bytes 9437184 | tf_op jit(solution)/shard_map/reduce_scatter | solution.py:86
  175.3 4.9 %copy-start.8 = (bf16[4,1536,512]{2,1,0:T(8,128)(2,1)S(1)}, bf16[4,1536,512]{2,1,0:T(8,128)(2,1)}, u32[]{:S(2)}) copy-start(bf16[4,1536,512]{2,1,0:T(8,128)(2,1)} %all-gather.12.cloned.1.call-done) | copy-start | bytes 18874372
  175.3 6.6 %copy-start.9 = (bf16[2048,1536]{1,0:T(8,128)(2,1)S(1)}, bf16[2048,1536]{1,0:T(8,128)(2,1)}, u32[]{:S(2)}) copy-start(bf16[2048,1536]{1,0:T(8,128)(2,1)} %all-gather.10.cloned.1.call-done) | copy-start | bytes 18874372
  232.0 1.1 copy-start.1
  232.0 1.2 copy-start.4
  232.0 37.7 %all-reduce.2.cloned.1.call-start = ((), (), s32[]{:S(2)}) async-start(), calls=%async_computation.7 | async-start | bytes 524288 | tf_op jit(solution)/shard_map/psum | solution.py:59
  234.3 9.0 %copy-start.2 = (bf16[512,1536]{1,0:T(8,128)(2,1)S(1)}, bf16[512,1536]{1,0:T(8,128)(2,1)}, u32[]{:S(2)}) copy-start(bf16[512,1536]{1,0:T(8,128)(2,1)} %all-gather.6.cloned.1.call-done) | copy-start | bytes 4718596
  234.3 47.9 %reduce-scatter.4.cloned.1.call-start = ((), (), s32[]{:S(2)}) async-start(), calls=%async_computation.6 | async-start | bytes 2359296 | tf_op jit(solution)/shard_map/reduce_scatter | solution.py:75
  250.8 0.8 copy-start.11
  250.8 1.0 copy-start.7
  250.8 94.6 %copy-start.10 = (bf16[256,768]{1,0:T(8,128)(2,1)S(1)}, bf16[256,768]{1,0:T(8,128)(2,1)}, u32[]{:S(2)}) copy-start(bf16[256,768]{1,0:T(8,128)(2,1)} %param.14) | copy-start | bytes 1179652
  250.8 94.5 %reduce-scatter.8.cloned.1.call-start = ((), (), s32[]{:S(2)}) async-start(), calls=%async_computation.13 | async-start | bytes 3932160 | tf_op jit(solution)/shard_map/reduce_scatter | solution.py:87
Sparse Core Ops, SparseCore 0:
  8.9 62.2 all-gather.7
  72.8 10.9 all-gather.5
  85.7 70.1 all-gather.11
  157.3 17.9 all-gather.9
  176.9 43.9 all-gather.13
  232.1 15.6 reduce-scatter.5
  250.3 19.4 all-reduce.1
  272.0 10.2 reduce-scatter.3
  284.7 60.6 reduce-scatter.7

commit v2 on v1

--- a/solution.py
+++ b/solution.py
@@ -1,10 +1,174 @@
 import jax
 import jax.numpy as jnp
 from jax import lax
+from jax.experimental import pallas as pl
+from jax.experimental.pallas import tpu as pltpu
 from jax.sharding import PartitionSpec as P
 
 RANK = 16
 DEPTH = 4
+
+
+def gather_kernel(x, gu, down, x_all, gu_all, down_all, local, tok_send, tok_recv, w_send, w_recv):
+    req, c = lax.axis_index("req"), lax.axis_index("blk")
+    z, p = req // 4, req % 4
+    px = (p // 2) * 2 + 1 - p % 2
+    py = (1 - p // 2) * 2 + p % 2
+    pd = (1 - p // 2) * 2 + 1 - p % 2
+    s = 1 - c
+    rows, width = x.shape
+    dev = lambda r, b: {"device_id": (r, b), "device_id_type": pl.DeviceIdType.MESH}
+    rx, ry = z * 4 + px, z * 4 + py
+
+    barrier = pltpu.get_barrier_semaphore()
+    signal = lambda r, b: pl.semaphore_signal(barrier, inc=1, **dev(r, b))
+    signal(req, s)
+    for b in range(2):
+        signal(rx, b)
+        signal(ry, b)
+
+    @pl.when(z > 0)
+    def _():
+        signal(req - 4, c)
+
+    @pl.when(z < 3)
+    def _():
+        signal(req + 4, c)
+
+    pl.semaphore_wait(barrier, 5 + jnp.where(z > 0, 1, 0) + jnp.where(z < 3, 1, 0))
+
+    def place(zz, b):
+        return x_all.at[
+            pl.ds(pl.multiple_of(zz * rows, rows), rows), pl.ds(pl.multiple_of(b * width, width), width)
+        ]
+
+    def tok(src, zz, k_send, k_recv, r, b):
+        return pltpu.make_async_remote_copy(
+            src_ref=src, dst_ref=place(zz, c), send_sem=tok_send.at[k_send], recv_sem=tok_recv.at[k_recv], **dev(r, b)
+        )
+
+    def weights(src_gu, src_down, owner, part, k_send, rel, r, b):
+        return (
+            pltpu.make_async_remote_copy(
+                src_ref=src_gu, dst_ref=gu_all.at[owner, part], send_sem=w_send.at[0, k_send],
+                recv_sem=w_recv.at[0, rel, part], **dev(r, b)
+            ),
+            pltpu.make_async_remote_copy(
+                src_ref=src_down, dst_ref=down_all.at[part, owner], send_sem=w_send.at[1, k_send],
+                recv_sem=w_recv.at[1, rel, part], **dev(r, b)
+            ),
+        )
+
+    up = lambda d: tok(x if d == 0 else place(z - d, c), z - d, d, d, req + 4, c)
+    dn = lambda d: tok(x if d == 0 else place(z + d, c), z + d, 3 + d, 3 + d, req - 4, c)
+    sib_own = tok(x, z, 6, 6, req, s)
+    sib_up = lambda d: tok(place(z - d, c), z - d, 6 + d, 6 + d, req, s)
+    sib_dn = lambda d: tok(place(z + d, c), z + d, 9 + d, 9 + d, req, s)
+
+    pl.when(z < 3)(lambda: up(0).start())
+    pl.when(z > 0)(lambda: dn(0).start())
+
+    sends = []
+    for k, (r, rel) in enumerate(((rx, 1), (ry, 2))):
+        for t in range(2):
+            sends += list(weights(gu.at[t], down.at[t], p, c, 2 * k + t, rel, r, t))
+    for copy in sends:
+        copy.start()
+    own = weights(gu.at[s], down.at[s], p, c, 4, 0, req, s)
+    for copy in own:
+        copy.start()
+    sib_own.start()
+    here = (
+        pltpu.make_async_copy(x, place(z, c), local.at[0]),
+        pltpu.make_async_copy(gu.at[c], gu_all.at[p, c], local.at[1]),
+        pltpu.make_async_copy(down.at[c], down_all.at[c, p], local.at[2]),
+    )
+    for copy in here:
+        copy.start()
+
+    for d in range(1, 4):
+
+        @pl.when(z >= d)
+        def _():
+            up(d - 1).wait_recv()
+            if d < 3:
+                pl.when(z < 3)(lambda: up(d).start())
+            sib_up(d).start()
+
+        @pl.when(z + d <= 3)
+        def _():
+            dn(d - 1).wait_recv()
+            if d < 3:
+                pl.when(z > 0)(lambda: dn(d).start())
+            sib_dn(d).start()
+
+    def arrived(owner, part, rel):
+        for copy in weights(gu_all.at[owner, part], down_all.at[part, owner], owner, part, 0, rel, req, s):
+            copy.wait_recv()
+
+    arrived(px, 0, 1)
+    fwd_y = weights(gu_all.at[px, 0], down_all.at[0, px], px, 0, 5, 3, ry, c)
+    for copy in fwd_y:
+        copy.start()
+    arrived(py, 1, 2)
+    fwd_x = weights(gu_all.at[py, 1], down_all.at[1, py], py, 1, 6, 3, rx, c)
+    for copy in fwd_x:
+        copy.start()
+    arrived(px, 1, 1)
+    arrived(py, 0, 2)
+    for copy in weights(gu.at[s], down.at[s], p, s, 4, 0, req, s):
+        copy.wait_recv()
+    arrived(pd, 0, 3)
+    arrived(pd, 1, 3)
+    for copy in here:
+        copy.wait()
+    for copy in sends:
+        copy.wait_send()
+    for copy in own + fwd_y + fwd_x:
+        copy.wait_send()
+    sib_own.wait()
+    for d in range(1, 4):
+
+        @pl.when(z >= d)
+        def _():
+            sib_up(d).wait()
+
+        @pl.when(z + d <= 3)
+        def _():
+            sib_dn(d).wait()
+
+    for d in range(3):
+
+        @pl.when((z >= d) & (z < 3))
+        def _():
+            up(d).wait_send()
+
+        @pl.when((z + d <= 3) & (z > 0))
+        def _():
+            dn(d).wait_send()
+
+
+def gather(x, gu, down):
+    rows, width = x.shape
+    any_space = pl.BlockSpec(memory_space=pl.ANY)
+    return pl.pallas_call(
+        gather_kernel,
+        out_shape=(
+            jax.ShapeDtypeStruct((4 * rows, 2 * width), x.dtype),
+            jax.ShapeDtypeStruct((4,) + gu.shape, x.dtype),
+            jax.ShapeDtypeStruct((2, 4) + down.shape[1:], x.dtype),
+        ),
+        in_specs=[any_space] * 3,
+        out_specs=(any_space,) * 3,
+        scratch_shapes=[
+            pltpu.SemaphoreType.DMA((3,)),
+            pltpu.SemaphoreType.DMA((13,)),
+            pltpu.SemaphoreType.DMA((13,)),
+            pltpu.SemaphoreType.DMA((2, 7)),
+            pltpu.SemaphoreType.DMA((2, 4, 2)),
+        ],
+        compiler_params=pltpu.CompilerParams(collective_id=0, has_side_effects=True),
+    )(x, gu, down)
 
 
 def body(
@@ -33,26 +197,30 @@
     my_z = lax.axis_index("req") // plane
 
     gu = expert_gate_up[0].reshape(feat_local, 2, 2, half).transpose(2, 0, 1, 3)
-    gu = gu.reshape(2 * feat_local, 2 * half)
-    gu = lax.all_to_all(gu, "blk", split_axis=0, concat_axis=0, tiled=True)
-    down = lax.all_to_all(expert_down[0], "blk", split_axis=0, concat_axis=1, tiled=True)
-    gu_all = lax.all_gather(gu, "req", axis_index_groups=planes)
-    down_all = lax.all_gather(down, "req", axis_index_groups=planes)
-
-    x_half = lax.all_gather(normed, "req", axis_index_groups=columns, tiled=True)
-    x_own = lax.all_gather(normed, "blk", axis=1, tiled=True)
-    x_all = lax.all_gather(x_half, "blk", axis=1, tiled=True)
-
+    gu = gu.reshape(2, feat_local, 2 * half)
+    down = expert_down[0].reshape(2, half, feat_local)
+    routes_all = lax.all_gather(routes, "req", axis_index_groups=columns, tiled=True)
     router_full = lax.all_gather(router, "blk", axis=0, tiled=True)
-    logits = jnp.dot(x_own, router_full, preferred_element_type=f32)
+    if plane == 4:
+        x_all, gu_all, down_all = gather(normed, gu, down)
+        gu_all = gu_all.reshape(plane, feat, 2 * half)
+    else:
+        gu = lax.all_to_all(gu, "blk", split_axis=0, concat_axis=0).reshape(feat, 2 * half)
+        down = lax.all_to_all(down, "blk", split_axis=0, concat_axis=0)
+        gu_all = lax.all_gather(gu, "req", axis_index_groups=planes)
+        down_all = lax.all_gather(down, "req", axis=1, axis_index_groups=planes)
+        x_half = lax.all_gather(normed, "req", axis_index_groups=columns, tiled=True)
+        x_all = lax.all_gather(x_half, "blk", axis=1, tiled=True)
+    x_own = lax.dynamic_slice_in_dim(x_all, my_z * tok_rows, tok_rows, axis=0)
+
+    logits = jnp.dot(x_all, router_full, preferred_element_type=f32)
     scores = jax.nn.sigmoid(logits)
     experts = jnp.arange(expert_count, dtype=jnp.int32)
-    named = jnp.zeros((tok_rows, expert_count), jnp.bool_)
+    named = jnp.zeros(scores.shape, jnp.bool_)
     for k in range(routes.shape[1]):
-        named = named | (routes[:, k : k + 1] == experts[None, :])
+        named = named | (routes_all[:, k : k + 1] == experts[None, :])
     chosen = jnp.where(named, scores, 0.0)
-    gate = chosen / jnp.sum(chosen, axis=1, keepdims=True)
-    gate_all = lax.all_gather(gate, "req", axis_index_groups=columns, tiled=True)
+    gate_all = chosen / jnp.sum(chosen, axis=1, keepdims=True)
     gate_here = lax.dynamic_slice_in_dim(gate_all, my_z * plane, plane, axis=1)
 
     low_part = jnp.dot(normed, adapter_down, preferred_element_type=f32)
@@ -82,7 +250,13 @@
         up_p = jnp.dot(x_all, gu_all[p, :, half:], preferred_element_type=f32)
         pieces.append((jax.nn.silu(gate_p) * up_p * gate_here[:, p : p + 1]).astype(bf16))
     hidden = jnp.concatenate(pieces, axis=1)
-    terms = jnp.dot(hidden, down_all.reshape(plane * half, feat), preferred_element_type=f32)
+    terms = jnp.concatenate(
+        [
+            jnp.dot(hidden, down_all[b].reshape(plane * half, feat_local), preferred_element_type=f32)
+            for b in range(2)
+        ],
+        axis=1,
+    )
     terms = lax.psum_scatter(terms.astype(bf16), "blk", scatter_dimension=1, tiled=True)
     routed = lax.psum_scatter(
         terms, "req", scatter_dimension=0, axis_index_groups=columns, tiled=True

time: 357 us -> 290 us (0.81)
  waiting for transfers between devices: 253 us -> 91.9 us
  Pallas kernels: 0 us -> 78.2 us
  matrix products: 46.6 us -> 60.5 us
  blocking collectives: 24.9 us -> 18.8 us
  local copies, waits for them, and re-layouts: 16.7 us -> 21.2 us
    all_gather x5 -> x0, waiting for transfers between devices: 157 us -> none  [the longest x1 56.4 us: body(): gu_all = lax.all_gather(gu, 'req', axis_index_groups=planes)]
    pallas_call x0 -> x1, Pallas kernels: none -> 78.2 us  [gather(): pl.pallas_call(gather_kernel, out_shape=(jax.ShapeDtypeStruct((4 * rows,...]
    all_to_all x2 -> x0, blocking collectives: 9.36 us -> none  [the longest x1 5 us: body(): gu = lax.all_to_all(gu, 'blk', split_axis=0, concat_axis=0, tiled=True)]
    dot_general x4, matrix products: 10.5 us -> 19.3 us  [body(): gate_p = jnp.dot(x_all, gu_all[p, :, :half], preferred_element_type=f32)]
    another operation x0 -> x2, local copies, waits for them, and re-layouts: none -> 6.61 us  [body(): gu = expert_gate_up[0].reshape(feat_local, 2, 2, half).transpose(2, 0, 1, 3)]
    dot_general x4, matrix products: 11.8 us -> 15.4 us  [body(): up_p = jnp.dot(x_all, gu_all[p, :, half:], preferred_element_type=f32)]
    dot_general x2 -> x3, matrix products: 13 us -> 12.6 us  [the longest x2 7.89 us: body(): jnp.dot(hidden, down_all[b].reshape(plane * half, feat_local), preferred_...]
  transfers between devices with their start and end apart: 9 -> 4, of which waited for: 8 -> 3; matrix products, arithmetic and copies ran while one was open for 13% -> 7% of each run, Pallas kernels for 0% -> 0%
where the time goes in v2:
time: 290 us; the launch traced here: 288 us
  waiting for transfers between devices  91.9 us (32%)
  Pallas kernels  78.2 us (27%)
  matrix products  60.5 us (21%)
  local copies, waits for them, and re-layouts  21.2 us (7%)
  blocking collectives  18.8 us (6%)
  between operations  13.4 us (5%)
  other arithmetic  3.5 us (1%)
    pallas_call x1, Pallas kernels, gather(): pl.pallas_call(gather_kernel, out_shape=(jax.ShapeDtypeStruct((4 * rows,...  78.2 us
    reduce_scatter x1, waiting for transfers between devices, body(): lax.psum_scatter(terms, 'req', scatter_dimension=0, axis_index_groups=col...  63 us
    dot_general x4, matrix products, body(): gate_p = jnp.dot(x_all, gu_all[p, :, :half], preferred_element_type=f32)  19.3 us
    all_gather x1, blocking collectives, body(): lax.all_gather(routes, 'req', axis_index_groups=columns, tiled=True)  15.9 us
    psum x1, waiting for transfers between devices, body(): low_all = lax.psum(low_part.astype(bf16), 'blk').astype(f32)  15.8 us
    dot_general x4, matrix products, body(): up_p = jnp.dot(x_all, gu_all[p, :, half:], preferred_element_type=f32)  15.4 us
    reduce_scatter x1, waiting for transfers between devices, body(): lax.psum_scatter(shared_terms.astype(bf16), 'blk', scatter_dimension=1, t...  12.5 us
    slice x1, local copies, waits for them, and re-layouts, body(): shared_gate_up[:, 0, :]  9.58 us
  transfers between devices with their start and end apart: 4, of which 3 were waited for; matrix products, arithmetic and copies ran while one was open for 7% of the time, Pallas kernels for 0%

profile of v2, /device:TPU:14, one launch (start us, length us, event | category | flops | bytes accessed | tf_op | source)
XLA Modules:
  0.0 287.7 jit_solution(4308125883761478345)
XLA Ops:
  6.5 4.0 %reshape_squeeze.12 = bf16[768,2,2,256]{3,2,1,0:T(2,128)(2,1)} reshape(bf16[1,768,1024]{2,1,0:T(8,128)(2,1)} %param.17) | data formatting | bytes 3145728 | tf_op jit(solution)/shard_map/reshape;squeeze | solution.py:199
  10.5 2.6 copy.40
  13.2 2.3 reshape.46.gu
  15.5 78.2 %shard_map.109 = (bf16[2048,1536]{1,0:T(8,128)(2,1)}, bf16[4,2,768,512]{3,2,1,0:T(8,128)(2,1)}, bf16[2,4,256,768]{3,2,1,0:T(8,128)(2,1)}) custom-call(bf16[512,768]{1,0:T(8,128)(2,1)} %x.1, bf16[2,768,512]{2,1,0:T(8,128)(2,1)} %reshape.46.gu, bf16[2,256,768]{2,1,0:T(8,128)(2,1)} %bitcast.77), custom_call_target="tpu_custom_call" | custom-call | tf_op jit(solution)/shard_map/pallas_call | solution.py:154
  93.7 6.2 %fusion.27 = f32[2048,256]{0,1:T(8,128)} fusion(bf16[2048,1536]{1,0:T(8,128)(2,1)} %get-tuple-element.8, bf16[4,1536,512]{2,1,0:T(8,128)(2,1)} %bitcast.90), kind=kOutput, calls=%fused_computation.38 | convolution fusion | flops 1610612736 | bytes 9175040 | tf_op jit(solution)/shard_map/dot_general | solution.py:249
  100.0 0.0 copy-done.1
  100.0 4.3 %fusion.28 = f32[2048,256]{0,1:T(8,128)} fusion(bf16[2048,1536]{1,0:T(8,128)(2,1)S(1)} %copy-done.1, bf16[4,1536,512]{2,1,0:T(8,128)(2,1)} %bitcast.91), kind=kOutput, calls=%fused_computation.41 | convolution fusion | flops 1610612736 | bytes 9175040 | tf_op jit(solution)/shard_map/dot_general | solution.py:249
  104.2 4.3 %fusion.29 = f32[2048,256]{0,1:T(8,128)} fusion(bf16[2048,1536]{1,0:T(8,128)(2,1)S(1)} %copy-done.1, bf16[4,1536,512]{2,1,0:T(8,128)(2,1)} %bitcast.92), kind=kOutput, calls=%fused_computation.44 | convolution fusion | flops 1610612736 | bytes 9175040 | tf_op jit(solution)/shard_map/dot_general | solution.py:249
  108.6 4.5 %fusion.30 = f32[2048,256]{0,1:T(8,128)} fusion(bf16[2048,1536]{1,0:T(8,128)(2,1)S(1)} %copy-done.1, bf16[4,1536,512]{2,1,0:T(8,128)(2,1)} %bitcast.93), kind=kOutput, calls=%fused_computation.47 | convolution fusion | flops 1610612736 | bytes 9175040 | tf_op jit(solution)/shard_map/dot_general | solution.py:249
  113.0 1.4 fusion.48
  114.4 2.9 all_gather.7
  117.3 0.0 copy-done.7
  117.3 15.9 %all_gather.6 = s32[2048,6]{0,1:T(8,128)S(1)} all-gather(s32[512,6]{0,1:T(8,128)S(1)} %copy-done.7), channel_id=1, replica_groups={{0,8,16,24},{2,10,18,26},{4,12,20,28},{6,14,22,30},{1,9,17,25},{3,11,19..., dimensions={0}, use_global_device_ids=true | all-gather | bytes 61440 | tf_op jit(solution)/shard_map/all_gather | solution.py:202
  133.2 0.0 slice-start
  133.2 4.7 %fusion.51 = (f32[2048]{0:T(1024)S(1)}, f32[2048,16]{0,1:T(8,128)S(1)}) fusion(bf16[2048,1536]{1,0:T(8,128)(2,1)} %get-tuple-element.8, bf16[1536,16]{0,1:T(8,128)(2,1)S(1)} %all_gather.7, s32[2048]{0:T(1024)S(1)} %bitcast.79, s32[2048]{0:T(1024)S(1)} %bitcast.80, s32[2048]{0:T(1024)S(1)} %bitcast.81, s32[2048]{0:T(1024)S(1)} %bitcast.82, ...), kind=kOutput, calls=%fused_computation.83 | convolution fusion | flops 101185536 | bytes 6529024 | tf_op jit(solution)/shard_map/dot_general | solution.py:216
  138.0 0.0 slice-start.1
  138.0 5.2 %fusion.7 = bf16[2048,256]{0,1:T(8,128)(2,1)S(1)} fusion(bf16[2048,1536]{1,0:T(8,128)(2,1)} %get-tuple-element.8, f32[2048,256]{0,1:T(8,128)S(1)} %copy-done.14, f32[2048]{0:T(1024)S(1)} %bitcast.87, bf16[4,1536,512]{2,1,0:T(8,128)(2,1)} %bitcast.94), kind=kOutput, calls=%fused_computation.16 | convolution fusion | flops 1614282752 | bytes 10231808 | tf_op jit(solution)/shard_map/dot_general | solution.py:250
  143.2 0.0 slice-done
  143.3 0.0 slice-done.1
  143.3 0.0 copy-done.13
  143.3 3.4 %fusion.6 = bf16[2048,256]{0,1:T(8,128)(2,1)S(1)} fusion(bf16[2048,1536]{1,0:T(8,128)(2,1)S(1)} %bitcast.73, f32[2048,256]{0,1:T(8,128)S(1)} %copy-done.13, f32[2048]{0:T(1024)S(1)} %bitcast.86, bf16[4,1536,512]{2,1,0:T(8,128)(2,1)} %bitcast.95), kind=kOutput, calls=%fused_computation.15 | convolution fusion | flops 1614282752 | bytes 10231808 | tf_op jit(solution)/shard_map/dot_general | solution.py:250
  146.7 3.4 %fusion.5 = bf16[2048,256]{0,1:T(8,128)(2,1)S(1)} fusion(bf16[2048,1536]{1,0:T(8,128)(2,1)S(1)} %bitcast.73, f32[2048,256]{0,1:T(8,128)S(1)} %copy-done.12, f32[2048]{0:T(1024)S(1)} %bitcast.85, bf16[4,1536,512]{2,1,0:T(8,128)(2,1)} %bitcast.96), kind=kOutput, calls=%fused_computation.14 | convolution fusion | flops 1614282752 | bytes 10231808 | tf_op jit(solution)/shard_map/dot_general | solution.py:250
  150.2 3.4 %fusion.4 = bf16[2048,256]{0,1:T(8,128)(2,1)S(1)} fusion(bf16[2048,1536]{1,0:T(8,128)(2,1)S(1)} %bitcast.73, f32[2048,256]{0,1:T(8,128)S(1)} %copy-done.11, f32[2048]{0:T(1024)S(1)} %bitcast.84, bf16[4,1536,512]{2,1,0:T(8,128)(2,1)} %bitcast.97), kind=kOutput, calls=%fused_computation.13 | convolution fusion | flops 1614282752 | bytes 10231808 | tf_op jit(solution)/shard_map/dot_general | solution.py:250
  153.6 4.1 %convolution_convert_fusion = bf16[2048,768]{1,0:T(8,128)(2,1)S(1)} fusion(bf16[1024,768]{1,0:T(8,128)(2,1)S(1)} %bitcast.76, bf16[2048,256]{0,1:T(8,128)(2,1)S(1)} %fusion.7, bf16[2048,256]{0,1:T(8,128)(2,1)S(1)} %fusion.6, bf16[2048,256]{0,1:T(8,128)(2,1)S(1)} %fusion.5, bf16[2048,256]{0,1:T(8,128)(2,1)S(1)} %fusion.4), kind=kOutput, calls=%fused_computation.2 | convolution fusion | flops 3239575552 | bytes 8912896 | tf_op jit(solution)/shard_map/dot_general | solution.py:255
  157.6 3.8 %convolution_convert_fusion.1 = bf16[2048,768]{1,0:T(8,128)(2,1)S(1)} fusion(bf16[1024,768]{1,0:T(8,128)(2,1)S(1)} %bitcast.75, bf16[2048,256]{0,1:T(8,128)(2,1)S(1)} %fusion.7, bf16[2048,256]{0,1:T(8,128)(2,1)S(1)} %fusion.6, bf16[2048,256]{0,1:T(8,128)(2,1)S(1)} %fusion.5, bf16[2048,256]{0,1:T(8,128)(2,1)S(1)} %fusion.4), kind=kOutput, calls=%fused_computation.3 | convolution fusion | flops 3239575552 | bytes 8912896 | tf_op jit(solution)/shard_map/dot_general | solution.py:255
  161.5 3.1 %pad_maximum_fusion = bf16[2048,1536]{1,0:T(8,128)(2,1)} fusion(bf16[2048,768]{1,0:T(8,128)(2,1)S(1)} %convolution_convert_fusion, bf16[2048,768]{1,0:T(8,128)(2,1)S(1)} %convolution_convert_fusion.1), kind=kLoop, calls=%fused_computation | loop fusion | flops 12582912 | bytes 12582912 | tf_op jit(solution)/shard_map/concatenate | solution.py:253
  164.6 0.0 reduce-scatter.6.cloned.1.call-update
  164.6 0.0 all-reduce.2.cloned.1.call-start
  164.7 1.1 copy-done.3
  165.8 0.1 copy-done.5
  165.9 1.1 convolution_convert_fusion.3
  166.9 0.0 all-reduce.2.cloned.1.call-update
  167.0 0.0 reduce-scatter.4.cloned.1.call-start
  167.0 9.6 %fusion.47 = (bf16[1536,1,512]{2,1,0:T(2,128)(2,1)}, bf16[1536,1,512]{2,1,0:T(2,128)(2,1)}) fusion(bf16[1536,2,512]{2,1,0:T(2,128)(2,1)} %param.15), kind=kLoop, calls=%fused_computation.79 | loop fusion | bytes 6291456 | tf_op jit(solution)/shard_map/slice | solution.py:239
  176.6 3.9 %fusion.13 = f32[512,512]{1,0:T(8,128)S(1)} fusion(bf16[1536,1,512]{2,1,0:T(2,128)(2,1)} %get-tuple-element.11, bf16[2048,1536]{1,0:T(8,128)(2,1)} %get-tuple-element.8, s32[]{:T(128)S(6)} %select_n.33), kind=kOutput, calls=%fused_computation.25 | convolution fusion | flops 805306368 | bytes 5767172 | tf_op jit(solution)/shard_map/dot_general | solution.py:239
  180.5 5.4 %convolution_convert_fusion.2 = bf16[512,1536]{1,0:T(8,128)(2,1)} fusion(bf16[512,1536]{1,0:T(8,128)(2,1)S(1)} %copy-done, bf16[1536,1,512]{2,1,0:T(2,128)(2,1)} %get-tuple-element.12, bf16[2048,1536]{1,0:T(8,128)(2,1)} %get-tuple-element.8, s32[]{:T(128)S(6)} %select_n.33, f32[512,512]{1,0:T(8,128)S(1)} %fusion.13), kind=kOutput, calls=%fused_computation.4 | convolution fusion | flops 1612972032 | bytes 8912900 | tf_op jit(solution)/shard_map/dot_general | solution.py:242
  186.0 0.0 reduce-scatter.4.cloned.1.call-update
  186.0 0.0 reduce-scatter.8.cloned.1.call-start
  186.0 0.0 reduce-scatter.6.cloned.1.call-done
  186.1 0.5 reduce-scatter.8.cloned.1.call-update
  186.6 0.0 copy-done.10
  186.6 0.2 reduce-window.8
  186.8 0.1 convert_reduce_fusion
  186.9 0.1 select_reduce_fusion
  187.0 15.8 %all-reduce.2.cloned.1.call-done = bf16[512,256]{1,0:T(8,128)(2,1)} async-done(((bf16[512,256]{1,0:T(8,128)(2,1)}), bf16[512,256]{1,0:T(8,128)(2,1)}) %all-reduce.2.cloned.1.call-update) | async-done | bytes 262160 | tf_op jit(solution)/shard_map/psum | solution.py:227
  202.8 12.5 %reduce-scatter.4.cloned.1.call-done = bf16[512,768]{1,0:T(8,128)(2,1)} async-done(((bf16[512,1536]{1,0:T(8,128)(2,1)}), bf16[512,768]{1,0:T(8,128)(2,1)}) %reduce-scatter.4.cloned.1.call-update) | async-done | bytes 786448 | tf_op jit(solution)/shard_map/reduce_scatter | solution.py:243
  215.3 63.0 %reduce-scatter.8.cloned.1.call-done = bf16[512,768]{1,0:T(8,128)(2,1)} async-done(((bf16[2048,768]{1,0:T(8,128)(2,1)}), bf16[512,768]{1,0:T(8,128)(2,1)}) %reduce-scatter.8.cloned.1.call-update) | async-done | bytes 786448 | tf_op jit(solution)/shard_map/reduce_scatter | solution.py:261
  278.3 2.8 add_convert_fusion
  (30 shorter events, 0.1 us)
Async XLA Ops:
  6.5 174.0 %copy-start = (bf16[512,1536]{1,0:T(8,128)(2,1)S(1)}, bf16[512,1536]{1,0:T(8,128)(2,1)}, u32[]{:S(2)}) copy-start(bf16[512,1536]{1,0:T(8,128)(2,1)} %param.16) | copy-start | bytes 4718596
  6.5 179.5 %reduce-scatter.6.cloned.1.call-start = ((), (), s32[]{:S(2)}) async-start(), calls=%async_computation.5 | async-start | bytes 9437184 | tf_op jit(solution)/shard_map/reduce_scatter | solution.py:260
  93.7 6.2 %copy-start.1 = (bf16[2048,1536]{1,0:T(8,128)(2,1)S(1)}, bf16[2048,1536]{1,0:T(8,128)(2,1)}, u32[]{:S(2)}) copy-start(bf16[2048,1536]{1,0:T(8,128)(2,1)} %get-tuple-element.8) | copy-start | bytes 18874372
  108.6 4.5 %copy-start.2 = (bf16[2,4,256,768]{3,2,1,0:T(8,128)(2,1)S(1)}, bf16[2,4,256,768]{3,2,1,0:T(8,128)(2,1)}, u32[]{:S(2)}) copy-start(bf16[2,4,256,768]{3,2,1,0:T(8,128)(2,1)} %get-tuple-element.10) | copy-start | bytes 9437188
  113.0 1.4 copy-start.6
  113.0 4.2 %copy-start.7 = (s32[512,6]{0,1:T(8,128)S(1)}, s32[512,6]{0,1:T(8,128)}, u32[]{:S(2)}) copy-start(s32[512,6]{0,1:T(8,128)} %param.21) | copy-start | bytes 36868
  133.2 4.8 %copy-start.14 = (f32[2048,256]{0,1:T(8,128)S(1)}, f32[2048,256]{0,1:T(8,128)}, u32[]{:S(2)}) copy-start(f32[2048,256]{0,1:T(8,128)} %fusion.27) | copy-start | bytes 6291460
  133.2 10.0 %slice-start = ((s8[6291456]{0:T(1024)(128)(4,1)}), s8[4194304]{0:T(1024)(128)(4,1)S(1)}, s32[]{:S(2)}) async-start(s8[6291456]{0:T(1024)(128)(4,1)} %bitcast.72), calls=%async_computation.7 | async-start | bytes 8388608
  138.0 5.2 %slice-start.1 = ((s8[6291456]{0:T(1024)(128)(4,1)}), s8[2097152]{0:T(1024)(128)(4,1)S(1)}, s32[]{:S(2)}) async-start(s8[6291456]{0:T(1024)(128)(4,1)} %bitcast.72), calls=%async_computation.8 | async-start | bytes 4194304
  138.0 5.2 %copy-start.13 = (f32[2048,256]{0,1:T(8,128)S(1)}, f32[2048,256]{0,1:T(8,128)}, u32[]{:S(2)}) copy-start(f32[2048,256]{0,1:T(8,128)} %fusion.28) | copy-start | bytes 6291460
  143.3 3.4 %copy-start.12 = (f32[2048,256]{0,1:T(8,128)S(1)}, f32[2048,256]{0,1:T(8,128)}, u32[]{:S(2)}) copy-start(f32[2048,256]{0,1:T(8,128)} %fusion.29) | copy-start | bytes 6291460
  146.7 3.4 %copy-start.11 = (f32[2048,256]{0,1:T(8,128)S(1)}, f32[2048,256]{0,1:T(8,128)}, u32[]{:S(2)}) copy-start(f32[2048,256]{0,1:T(8,128)} %fusion.30) | copy-start | bytes 6291460
  150.2 3.4 %copy-start.4 = (bf16[1,4,256,768]{3,2,1,0:T(8,128)(2,1)S(1)}, bf16[1,4,256,768]{3,2,1,0:T(8,128)(2,1)}, u32[]{:S(2)}) copy-start(bf16[1,4,256,768]{3,2,1,0:T(8,128)(2,1)} %get-tuple-element.14) | copy-start | bytes 4718596
  164.6 1.1 copy-start.3
  164.6 1.2 copy-start.5
  164.6 38.1 %all-reduce.2.cloned.1.call-start = ((), (), s32[]{:S(2)}) async-start(), calls=%async_computation.4 | async-start | bytes 524288 | tf_op jit(solution)/shard_map/psum | solution.py:227
  167.0 48.4 %reduce-scatter.4.cloned.1.call-start = ((), (), s32[]{:S(2)}) async-start(), calls=%async_computation.3 | async-start | bytes 2359296 | tf_op jit(solution)/shard_map/reduce_scatter | solution.py:243
  185.9 0.7 copy-start.10
  186.0 0.9 copy-start.8
  186.0 92.3 %copy-start.9 = (bf16[256,768]{1,0:T(8,128)(2,1)S(1)}, bf16[256,768]{1,0:T(8,128)(2,1)}, u32[]{:S(2)}) copy-start(bf16[256,768]{1,0:T(8,128)(2,1)} %param.14) | copy-start | bytes 1179652
  186.0 92.3 %reduce-scatter.8.cloned.1.call-start = ((), (), s32[]{:S(2)}) async-start(), calls=%async_computation.6 | async-start | bytes 3932160 | tf_op jit(solution)/shard_map/reduce_scatter | solution.py:261
Sparse Core Ops, SparseCore 0:
  164.8 16.0 reduce-scatter.5
  183.3 19.4 all-reduce.1
  205.0 10.2 reduce-scatter.3
  217.6 60.6 reduce-scatter.7

commit v3 on v2

--- a/solution.py
+++ b/solution.py
@@ -9,7 +9,10 @@
 DEPTH = 4
 
 
-def gather_kernel(x, gu, down, x_all, gu_all, down_all, local, tok_send, tok_recv, w_send, w_recv):
+def gather_kernel(
+    x, gu, down, rt, ro, ad, x_all, gu_all, down_all, rt_all, ro_all, ad_all,
+    local, tok_send, tok_recv, w_send, w_recv, s_send, s_recv,
+):
     req, c = lax.axis_index("req"), lax.axis_index("blk")
     z, p = req // 4, req % 4
     px = (p // 2) * 2 + 1 - p % 2
@@ -27,15 +30,23 @@
         signal(rx, b)
         signal(ry, b)
 
-    @pl.when(z > 0)
-    def _():
-        signal(req - 4, c)
-
-    @pl.when(z < 3)
-    def _():
-        signal(req + 4, c)
-
-    pl.semaphore_wait(barrier, 5 + jnp.where(z > 0, 1, 0) + jnp.where(z < 3, 1, 0))
+    for d in range(1, 4):
+        signal(((z + d) % 4) * 4 + p, c)
+    pl.semaphore_wait(barrier, 8)
+    small = [
+        pltpu.make_async_remote_copy(
+            src_ref=rt, dst_ref=rt_all.at[z], send_sem=s_send.at[d - 1], recv_sem=s_recv.at[d - 1],
+            **dev(((z + d) % 4) * 4 + p, c)
+        )
+        for d in range(1, 4)
+    ] + [
+        pltpu.make_async_remote_copy(
+            src_ref=src, dst_ref=dst.at[c], send_sem=s_send.at[k], recv_sem=s_recv.at[k], **dev(req, s)
+        )
+        for k, src, dst in ((3, ro, ro_all), (4, ad, ad_all))
+    ]
+    for copy in small:
+        copy.start()
 
     def place(zz, b):
         return x_all.at[
@@ -82,6 +93,9 @@
         pltpu.make_async_copy(x, place(z, c), local.at[0]),
         pltpu.make_async_copy(gu.at[c], gu_all.at[p, c], local.at[1]),
         pltpu.make_async_copy(down.at[c], down_all.at[c, p], local.at[2]),
+        pltpu.make_async_copy(rt, rt_all.at[z], local.at[3]),
+        pltpu.make_async_copy(ro, ro_all.at[c], local.at[4]),
+        pltpu.make_async_copy(ad, ad_all.at[c], local.at[5]),
     )
     for copy in here:
         copy.start()
@@ -120,7 +134,7 @@
         copy.wait_recv()
     arrived(pd, 0, 3)
     arrived(pd, 1, 3)
-    for copy in here:
+    for copy in here + tuple(small):
         copy.wait()
     for copy in sends:
         copy.wait_send()
@@ -148,7 +162,7 @@
             dn(d).wait_send()
 
 
-def gather(x, gu, down):
+def gather(x, gu, down, rt, ro, ad):
     rows, width = x.shape
     any_space = pl.BlockSpec(memory_space=pl.ANY)
     return pl.pallas_call(
@@ -157,18 +171,171 @@
             jax.ShapeDtypeStruct((4 * rows, 2 * width), x.dtype),
             jax.ShapeDtypeStruct((4,) + gu.shape, x.dtype),
             jax.ShapeDtypeStruct((2, 4) + down.shape[1:], x.dtype),
+            jax.ShapeDtypeStruct((4,) + rt.shape, rt.dtype),
+            jax.ShapeDtypeStruct((2,) + ro.shape, ro.dtype),
+            jax.ShapeDtypeStruct((2,) + ad.shape, ad.dtype),
         ),
-        in_specs=[any_space] * 3,
-        out_specs=(any_space,) * 3,
+        in_specs=[any_space] * 6,
+        out_specs=(any_space,) * 6,
         scratch_shapes=[
-            pltpu.SemaphoreType.DMA((3,)),
+            pltpu.SemaphoreType.DMA((6,)),
             pltpu.SemaphoreType.DMA((13,)),
             pltpu.SemaphoreType.DMA((13,)),
             pltpu.SemaphoreType.DMA((2, 7)),
             pltpu.SemaphoreType.DMA((2, 4, 2)),
+            pltpu.SemaphoreType.DMA((5,)),
+            pltpu.SemaphoreType.DMA((5,)),
         ],
         compiler_params=pltpu.CompilerParams(collective_id=0, has_side_effects=True),
-    )(x, gu, down)
+    )(x, gu, down, rt, ro, ad)
+
+
+def return_kernel(t, sh, out, sib, below, above, sh_in, sib_send, sib_recv, z_send, up_recv, dn_recv):
+    req, c = lax.axis_index("req"), lax.axis_index("blk")
+    z, s = req // 4, 1 - c
+    rows = sh.shape[1]
+    step = rows // 4
+    dev = lambda r, b: {"device_id": (r, b), "device_id_type": pl.DeviceIdType.MESH}
+    barrier = pltpu.get_barrier_semaphore()
+    pl.semaphore_signal(barrier, inc=1, **dev(req, s))
+
+    @pl.when(z > 0)
+    def _():
+        pl.semaphore_signal(barrier, inc=1, **dev(req - 4, c))
+
+    @pl.when(z < 3)
+    def _():
+        pl.semaphore_signal(barrier, inc=1, **dev(req + 4, c))
+
+    pl.semaphore_wait(barrier, 1 + jnp.where(z > 0, 1, 0) + jnp.where(z < 3, 1, 0))
+
+    def pair(src, dst, k):
+        return pltpu.make_async_remote_copy(
+            src_ref=src, dst_ref=dst, send_sem=sib_send.at[k], recv_sem=sib_recv.at[k], **dev(req, s)
+        )
+
+    def chain(k, dst, recv, r):
+        return pltpu.make_async_remote_copy(
+            src_ref=sib.at[k], dst_ref=dst.at[k], send_sem=z_send.at[k], recv_sem=recv.at[k], **dev(r, c)
+        )
+
+    order = (3, 0, 2, 1)
+    across = {k: pair(t.at[s, k], sib.at[k], k) for k in order}
+    across[4] = pair(sh.at[s], sh_in, 4)
+    for copy in across.values():
+        copy.start()
+
+    def add_into(k, other):
+        def one(i, carry):
+            at = pl.ds(pl.multiple_of(i * step, step), step)
+            sib[k, at, :] = (sib[k, at, :].astype(jnp.float32) + other(at).astype(jnp.float32)).astype(sib.dtype)
+            return carry
+
+        lax.fori_loop(0, 4, one, 0)
+
+    def add_pair(k, other):
+        def one(i, carry):
+            at = pl.ds(pl.multiple_of(i * step, step), step)
+            total = sib[k, at, :].astype(jnp.float32) + t[c, k, at, :].astype(jnp.float32)
+            sib[k, at, :] = (total + other[k, at, :].astype(jnp.float32)).astype(sib.dtype)
+            return carry
+
+        lax.fori_loop(0, 4, one, 0)
+
+    for k in order:
+        across[k].wait_recv()
+
+        if k > 0:
+
+            @pl.when((z < k) & (z > 0))
+            def _():
+                chain(k, below, up_recv, req + 4).wait_recv()
+                add_pair(k, below)
+
+            @pl.when((z < k) & (z == 0))
+            def _():
+                add_into(k, lambda at: t[c, k, at, :])
+
+            @pl.when(z < k)
+            def _():
+                chain(k, below, up_recv, req + 4).start()
+
+        if k < 3:
+
+            @pl.when((z > k) & (z < 3))
+            def _():
+                chain(k, above, dn_recv, req - 4).wait_recv()
+                add_pair(k, above)
+
+            @pl.when((z > k) & (z == 3))
+            def _():
+                add_into(k, lambda at: t[c, k, at, :])
+
+            @pl.when(z > k)
+            def _():
+                chain(k, above, dn_recv, req - 4).start()
+
+    across[4].wait_recv()
+    f32 = jnp.float32
+
+    def first(i, carry):
+        at = pl.ds(pl.multiple_of(i * step, step), step)
+        total = sib[z, at, :].astype(f32) + t[c, z, at, :].astype(f32)
+        out[at, :] = total + sh[c, at, :].astype(f32) + sh_in[at, :].astype(f32)
+        return carry
+
+    lax.fori_loop(0, 4, first, 0)
+
+    def more(buffer):
+        def one(i, carry):
+            at = pl.ds(pl.multiple_of(i * step, step), step)
+            out[at, :] += buffer[z, at, :].astype(f32)
+            return carry
+
+        lax.fori_loop(0, 4, one, 0)
+
+    @pl.when(z > 0)
+    def _():
+        chain(z, below, up_recv, req + 4).wait_recv()
+        more(below)
+
+    @pl.when(z < 3)
+    def _():
+        chain(z, above, dn_recv, req - 4).wait_recv()
+        more(above)
+
+    for copy in across.values():
+        copy.wait_send()
+    for k in order:
+
+        @pl.when(z != k)
+        def _():
+            chain(k, below, up_recv, req + 4).wait_send()
+
+
+def give_back(t, sh):
+    block = t.shape[1:]
+    vmem = pl.BlockSpec(memory_space=pltpu.VMEM)
+    return pl.pallas_call(
+        return_kernel,
+        out_shape=jax.ShapeDtypeStruct(block[1:], jnp.float32),
+        in_specs=[vmem, vmem],
+        out_specs=vmem,
+        scratch_shapes=[
+            pltpu.VMEM(block, t.dtype),
+            pltpu.VMEM(block, t.dtype),
+            pltpu.VMEM(block, t.dtype),
+            pltpu.VMEM(block[1:], t.dtype),
+            pltpu.SemaphoreType.DMA((5,)),
+            pltpu.SemaphoreType.DMA((5,)),
+            pltpu.SemaphoreType.DMA((4,)),
+            pltpu.SemaphoreType.DMA((4,)),
+            pltpu.SemaphoreType.DMA((4,)),
+        ],
+        compiler_params=pltpu.CompilerParams(
+            collective_id=1, has_side_effects=True, vmem_limit_bytes=48 * 1024 * 1024
+        ),
+    )(t, sh)
 
 
 def body(
@@ -199,12 +366,18 @@
     gu = expert_gate_up[0].reshape(feat_local, 2, 2, half).transpose(2, 0, 1, 3)
     gu = gu.reshape(2, feat_local, 2 * half)
     down = expert_down[0].reshape(2, half, feat_local)
-    routes_all = lax.all_gather(routes, "req", axis_index_groups=columns, tiled=True)
-    router_full = lax.all_gather(router, "blk", axis=0, tiled=True)
     if plane == 4:
-        x_all, gu_all, down_all = gather(normed, gu, down)
+        x_all, gu_all, down_all, routes_all, router_full, adapter_full = gather(
+            normed, gu, down, routes.T, router, adapter_down
+        )
+        routes_all = routes_all.transpose(0, 2, 1).reshape(DEPTH * tok_rows, routes.shape[1])
+        router_full = router_full.reshape(feat, expert_count)
+        adapter_full = adapter_full.reshape(feat, adapter_down.shape[1])
         gu_all = gu_all.reshape(plane, feat, 2 * half)
     else:
+        routes_all = lax.all_gather(routes, "req", axis_index_groups=columns, tiled=True)
+        router_full = lax.all_gather(router, "blk", axis=0, tiled=True)
+        adapter_full = lax.all_gather(adapter_down, "blk", axis=0, tiled=True)
         gu = lax.all_to_all(gu, "blk", split_axis=0, concat_axis=0).reshape(feat, 2 * half)
         down = lax.all_to_all(down, "blk", split_axis=0, concat_axis=0)
         gu_all = lax.all_gather(gu, "req", axis_index_groups=planes)
@@ -223,8 +396,7 @@
     gate_all = chosen / jnp.sum(chosen, axis=1, keepdims=True)
     gate_here = lax.dynamic_slice_in_dim(gate_all, my_z * plane, plane, axis=1)
 
-    low_part = jnp.dot(normed, adapter_down, preferred_element_type=f32)
-    low_all = lax.psum(low_part.astype(bf16), "blk").astype(f32)
+    low_all = jnp.dot(x_own, adapter_full, preferred_element_type=f32)
     ends = jnp.cumsum(lengths[0])
     position = jnp.arange(tok_rows, dtype=jnp.int32)
     request = jnp.sum((position[:, None] >= ends[None, :]).astype(jnp.int32), axis=1)
@@ -240,28 +412,28 @@
     shared_up = jnp.dot(x_own, shared_gate_up[:, 1, :], preferred_element_type=f32)
     shared_hidden = (jax.nn.silu(shared_gate) * shared_up).astype(bf16)
     shared_terms = jnp.dot(shared_hidden, shared_down, preferred_element_type=f32)
-    shared_out = lax.psum_scatter(
-        shared_terms.astype(bf16), "blk", scatter_dimension=1, tiled=True
-    ).astype(f32)
-
     pieces = []
     for p in range(plane):
         gate_p = jnp.dot(x_all, gu_all[p, :, :half], preferred_element_type=f32)
         up_p = jnp.dot(x_all, gu_all[p, :, half:], preferred_element_type=f32)
         pieces.append((jax.nn.silu(gate_p) * up_p * gate_here[:, p : p + 1]).astype(bf16))
     hidden = jnp.concatenate(pieces, axis=1)
-    terms = jnp.concatenate(
-        [
-            jnp.dot(hidden, down_all[b].reshape(plane * half, feat_local), preferred_element_type=f32)
-            for b in range(2)
-        ],
-        axis=1,
-    )
-    terms = lax.psum_scatter(terms.astype(bf16), "blk", scatter_dimension=1, tiled=True)
-    routed = lax.psum_scatter(
-        terms, "req", scatter_dimension=0, axis_index_groups=columns, tiled=True
-    ).astype(f32)
-    return (shared_out + 0.5 * delta + routed).astype(bf16)
+    terms = [
+        jnp.dot(hidden, down_all[b].reshape(plane * half, feat_local), preferred_element_type=f32).astype(bf16)
+        for b in range(2)
+    ]
+    shared_terms = shared_terms.astype(bf16)
+    if plane == 4:
+        parts = jnp.stack([x.reshape(DEPTH, tok_rows, feat_local) for x in terms])
+        shared_parts = jnp.stack([shared_terms[:, :feat_local], shared_terms[:, feat_local:]])
+        summed = give_back(parts, shared_parts)
+    else:
+        shared_out = lax.psum_scatter(shared_terms, "blk", scatter_dimension=1, tiled=True)
+        terms = lax.psum_scatter(jnp.concatenate(terms, axis=1), "blk", scatter_dimension=1, tiled=True)
+        summed = shared_out.astype(f32) + lax.psum_scatter(
+            terms, "req", scatter_dimension=0, axis_index_groups=columns, tiled=True
+        ).astype(f32)
+    return (summed + 0.5 * delta).astype(bf16)
 
 
 def solution(mesh):

time: 290 us -> 241 us (0.83)
  waiting for transfers between devices: 91.9 us -> 0 us
  Pallas kernels: 78.2 us -> 163 us
  blocking collectives: 18.8 us -> 0 us
  between operations: 13.4 us -> 0.32 us
  matrix products: 60.5 us -> 50.4 us
    pallas_call x0 -> x1, Pallas kernels: none -> 80.6 us  [give_back(): pl.pallas_call(return_kernel, out_shape=jax.ShapeDtypeStruct(block[1:], j...]
    reduce_scatter x3 -> x0, waiting for transfers between devices: 75.5 us -> none  [the longest x1 63 us: body(): lax.psum_scatter(terms, 'req', scatter_dimension=0, axis_index_groups=col...]
    all_gather x2 -> x0, blocking collectives: 18.8 us -> none  [the longest x1 15.9 us: body(): lax.all_gather(routes, 'req', axis_index_groups=columns, tiled=True)]
    psum x1 -> x0, waiting for transfers between devices: 15.8 us -> none  [body(): low_all = lax.psum(low_part.astype(bf16), 'blk').astype(f32)]
    dot_general x4, matrix products: 19.3 us -> 13 us  [body(): gate_p = jnp.dot(x_all, gu_all[p, :, :half], preferred_element_type=f32)]
    pallas_call x1, Pallas kernels: 78.2 us -> 82.3 us  [gather(): pl.pallas_call(gather_kernel, out_shape=(jax.ShapeDtypeStruct((4 * rows,...]
    slice x1, local copies, waits for them, and re-layouts: 9.58 us -> 5.9 us  [body(): shared_gate_up[:, 0, :]]
    another operation x1 -> x3, other arithmetic: 0.18 us -> 3.5 us  [the longest x1 3.18 us: body(): parts = jnp.stack([x.reshape(DEPTH, tok_rows, feat_local) for x in terms])]
  transfers between devices with their start and end apart: 4 -> 0, of which waited for: 3 -> 0; matrix products, arithmetic and copies ran while one was open for 7% -> 0% of each run, Pallas kernels for 0% -> 0%
where the time goes in v3:
time: 241 us; the launch traced here: 238 us
  Pallas kernels  163 us (68%)
  matrix products  50.4 us (21%)
  local copies, waits for them, and re-layouts  20.2 us (8%)
  other arithmetic  3.7 us (2%)
    pallas_call x1, Pallas kernels, gather(): pl.pallas_call(gather_kernel, out_shape=(jax.ShapeDtypeStruct((4 * rows,...  82.3 us
    pallas_call x1, Pallas kernels, give_back(): pl.pallas_call(return_kernel, out_shape=jax.ShapeDtypeStruct(block[1:], j...  80.6 us
    dot_general x4, matrix products, body(): up_p = jnp.dot(x_all, gu_all[p, :, half:], preferred_element_type=f32)  15.5 us
    dot_general x4, matrix products, body(): gate_p = jnp.dot(x_all, gu_all[p, :, :half], preferred_element_type=f32)  13 us
    dot_general x2, matrix products, body(): jnp.dot(hidden, down_all[b].reshape(plane * half, feat_local), preferred_...  7.75 us
    another operation x2, local copies, waits for them, and re-layouts, body(): gu = expert_gate_up[0].reshape(feat_local, 2, 2, half).transpose(2, 0, 1, 3)  6.62 us
    slice x1, local copies, waits for them, and re-layouts, body(): shared_gate_up[:, 0, :]  5.9 us

profile of v3, /device:TPU:14, one launch (start us, length us, event | category | flops | bytes accessed | tf_op | source)
XLA Modules:
  0.0 237.6 jit_solution(14928885161974131989)
XLA Ops:
  0.0 0.0 copy-start
  0.0 4.0 %reshape_squeeze.12 = bf16[768,2,2,256]{3,2,1,0:T(2,128)(2,1)} reshape(bf16[1,768,1024]{2,1,0:T(8,128)(2,1)} %param.17) | data formatting | bytes 3145728 | tf_op jit(solution)/shard_map/reshape;squeeze | solution.py:366
  4.0 2.6 %copy.35 = bf16[768,2,2,256]{3,1,0,2:T(2,128)(2,1)S(1)} copy(bf16[768,2,2,256]{3,2,1,0:T(2,128)(2,1)} %reshape_squeeze.12) | data formatting | bytes 3145728 | tf_op jit(solution)/shard_map/reshape;squeeze | solution.py:366
  6.6 2.3 reshape.55.gu
  8.9 0.0 copy-done.7
  8.9 0.8 copy.19.ro
  9.8 82.3 %shard_map.109 = (bf16[2048,1536]{1,0:T(8,128)(2,1)}, bf16[4,2,768,512]{3,2,1,0:T(8,128)(2,1)}, bf16[2,4,256,768]{3,2,1,0:T(8,128)(2,1)}, s32[4,6,512]{2,1,0:T(8...) custom-call(bf16[512,768]{1,0:T(8,128)(2,1)} %x.1, bf16[2,768,512]{2,1,0:T(8,128)(2,1)} %reshape.55.gu, ...), custom_call_target="tpu_custom_call" | custom-call | tf_op jit(solution)/shard_map/pallas_call | solution.py:168
  92.1 0.0 copy-start.1
  92.1 3.4 %fusion.51 = (bf16[1,4,256,768]{3,2,1,0:T(8,128)(2,1)S(1)}, bf16[1,4,256,768]{3,2,1,0:T(8,128)(2,1)}) fusion(bf16[2,4,256,768]{3,2,1,0:T(8,128)(2,1)} %get-tuple-element.15), kind=kLoop, calls=%fused_computation.86 | loop fusion | bytes 6291456 | tf_op jit(solution)/shard_map/slice | solution.py:422
  95.5 0.9 copy-done.1
  96.4 4.4 %fusion.27 = f32[2048,256]{0,1:T(8,128)} fusion(bf16[2048,1536]{1,0:T(8,128)(2,1)S(1)} %copy-done.1, bf16[4,1536,512]{2,1,0:T(8,128)(2,1)} %bitcast.107), kind=kOutput, calls=%fused_computation.43 | convolution fusion | flops 1610612736 | bytes 9175040 | tf_op jit(solution)/shard_map/dot_general | solution.py:417
  100.7 0.0 copy-done.6
  100.8 0.0 copy-done.4
  100.8 1.8 fusion.54
  102.7 5.7 %fusion.7 = bf16[2048,256]{0,1:T(8,128)(2,1)S(1)} fusion(bf16[2048,1536]{1,0:T(8,128)(2,1)} %get-tuple-element.11, f32[2048,256]{0,1:T(8,128)} %fusion.27, f32[2048]{0:T(1024)S(1)} %bitcast.104, bf16[4,1536,512]{2,1,0:T(8,128)(2,1)} %bitcast.108), kind=kOutput, calls=%fused_computation.16 | convolution fusion | flops 1614282752 | bytes 10231808 | tf_op jit(solution)/shard_map/dot_general | solution.py:418
  108.4 0.0 slice-start
  108.4 0.0 slice-start.2
  108.4 4.9 %fusion.28 = f32[2048,256]{0,1:T(8,128)S(1)} fusion(bf16[2048,1536]{1,0:T(8,128)(2,1)} %get-tuple-element.11, bf16[4,1536,512]{2,1,0:T(8,128)(2,1)} %bitcast.109), kind=kOutput, calls=%fused_computation.46 | convolution fusion | flops 1610612736 | bytes 9175040 | tf_op jit(solution)/shard_map/dot_general | solution.py:417
  113.3 0.0 slice-start.1
  113.4 0.0 slice-start.3
  113.4 5.2 %fusion.6 = bf16[2048,256]{0,1:T(8,128)(2,1)S(1)} fusion(bf16[2048,1536]{1,0:T(8,128)(2,1)} %get-tuple-element.11, f32[2048,256]{0,1:T(8,128)S(1)} %fusion.28, f32[2048]{0:T(1024)S(1)} %bitcast.103, bf16[4,1536,512]{2,1,0:T(8,128)(2,1)} %bitcast.110), kind=kOutput, calls=%fused_computation.15 | convolution fusion | flops 1614282752 | bytes 10231808 | tf_op jit(solution)/shard_map/dot_general | solution.py:418
  118.6 0.0 slice-done
  118.6 0.0 slice-done.2
  118.6 0.0 slice-done.1
  118.6 0.0 slice-done.3
  118.7 1.8 fusion.29
  120.5 2.4 fusion.5
  122.9 1.9 fusion.30
  124.7 0.0 copy-start.3
  124.8 2.1 fusion.4
  126.9 0.0 copy-done.3
  126.9 3.9 %convolution_convert_fusion = bf16[2048,768]{1,0:T(8,128)(2,1)S(1)} fusion(bf16[1024,768]{1,0:T(8,128)(2,1)S(1)} %bitcast.89, bf16[2048,256]{0,1:T(8,128)(2,1)S(1)} %fusion.7, bf16[2048,256]{0,1:T(8,128)(2,1)S(1)} %fusion.6, bf16[2048,256]{0,1:T(8,128)(2,1)S(1)} %fusion.5, bf16[2048,256]{0,1:T(8,128)(2,1)S(1)} %fusion.4), kind=kOutput, calls=%fused_computation.2 | convolution fusion | flops 3239575552 | bytes 8912896 | tf_op jit(solution)/shard_map/dot_general | solution.py:422
  130.8 3.9 %convolution_convert_fusion.1 = bf16[2048,768]{1,0:T(8,128)(2,1)S(1)} fusion(bf16[1024,768]{1,0:T(8,128)(2,1)S(1)} %bitcast.88, bf16[2048,256]{0,1:T(8,128)(2,1)S(1)} %fusion.7, bf16[2048,256]{0,1:T(8,128)(2,1)S(1)} %fusion.6, bf16[2048,256]{0,1:T(8,128)(2,1)S(1)} %fusion.5, bf16[2048,256]{0,1:T(8,128)(2,1)S(1)} %fusion.4), kind=kOutput, calls=%fused_computation.3 | convolution fusion | flops 3239575552 | bytes 8912896 | tf_op jit(solution)/shard_map/dot_general | solution.py:422
  134.7 0.0 copy-start.2
  134.7 3.2 %pad_maximum_fusion.t = bf16[2,4,512,768]{3,2,1,0:T(8,128)(2,1)} fusion(bf16[1,4,512,768]{3,2,1,0:T(8,128)(2,1)S(1)} %bitcast.86, bf16[1,4,512,768]{3,2,1,0:T(8,128)(2,1)S(1)} %bitcast.87), kind=kLoop, calls=%fused_computation | loop fusion | flops 3145728 | bytes 12582912 | tf_op jit(solution)/shard_map/stack | solution.py:427
  137.9 5.9 %fusion.50 = (bf16[1536,1,512]{2,1,0:T(2,128)(2,1)}, bf16[1536,1,512]{2,1,0:T(2,128)(2,1)}) fusion(bf16[1536,2,512]{2,1,0:T(2,128)(2,1)S(1)} %copy-done.2), kind=kLoop, calls=%fused_computation.85 | loop fusion | bytes 6291456 | tf_op jit(solution)/shard_map/slice | solution.py:411
  143.8 4.3 %fusion.13 = f32[512,512]{1,0:T(8,128)} fusion(bf16[1536,1,512]{2,1,0:T(2,128)(2,1)} %get-tuple-element.17, bf16[2048,1536]{1,0:T(8,128)(2,1)} %get-tuple-element.11, s32[]{:T(128)S(6)} %select_n.35), kind=kOutput, calls=%fused_computation.26 | convolution fusion | flops 805306368 | bytes 5767172 | tf_op jit(solution)/shard_map/dot_general | solution.py:411
  148.1 4.5 %convolution_convert_fusion.2 = bf16[512,1536]{1,0:T(8,128)(2,1)S(1)} fusion(bf16[512,1536]{1,0:T(8,128)(2,1)S(1)} %copy-done, bf16[1536,1,512]{2,1,0:T(2,128)(2,1)} %get-tuple-element.18, bf16[2048,1536]{1,0:T(8,128)(2,1)} %get-tuple-element.11, s32[]{:T(128)S(6)} %select_n.35, f32[512,512]{1,0:T(8,128)} %fusion.13), kind=kOutput, calls=%fused_computation.4 | convolution fusion | flops 1612972032 | bytes 8912900 | tf_op jit(solution)/shard_map/dot_general | solution.py:414
  152.6 0.1 slice_bitcast_fusion.1
  152.7 0.1 pad_maximum_fusion.2.sh
  152.9 0.0 copy-start.9
  152.9 0.0 copy-start.8
  152.9 0.0 copy-start.5
  152.9 80.6 %shard_map.110 = f32[512,768]{1,0:T(8,128)S(1)} custom-call(bf16[2,4,512,768]{3,2,1,0:T(8,128)(2,1)} %pad_maximum_fusion.t, bf16[2,512,768]{2,1,0:T(8,128)(2,1)S(1)} %pad_maximum_fusion.2.sh), custom_call_target="tpu_custom_call" | custom-call | tf_op jit(solution)/shard_map/pallas_call | solution.py:319
  233.6 0.2 reduce-window.8
  233.7 0.1 convert_reduce_fusion
  233.8 0.1 select_reduce_fusion
  233.9 3.6 %add_convert_fusion = bf16[512,768]{1,0:T(8,128)(2,1)} fusion(f32[512,768]{1,0:T(8,128)S(1)} %shard_map.110, bf16[256,768]{1,0:T(8,128)(2,1)S(1)} %copy-done.5, bf16[1536,256]{1,0:T(8,128)(2,1)} %bitcast.91, bf16[2048,1536]{1,0:T(8,128)(2,1)} %get-tuple-element.11, s32[]{:T(128)S(6)} %select_n.35, s32[256]{0:T(256)S(1)} %and_select_fusion, ...), kind=kOutput, calls=%fused_computation.28 | convolution fusion | flops 605552640 | bytes 5114884 | tf_op jit(solution)/shard_map/dot_general | solution.py:409
  (14 shorter events, 0.1 us)
Async XLA Ops:
  0.0 148.1 %copy-start = (bf16[512,1536]{1,0:T(8,128)(2,1)S(1)}, bf16[512,1536]{1,0:T(8,128)(2,1)}, u32[]{:S(2)}) copy-start(bf16[512,1536]{1,0:T(8,128)(2,1)} %param.16) | copy-start | bytes 4718596
  4.0 5.0 %copy-start.7 = (bf16[768,16]{0,1:T(8,128)(2,1)S(1)}, bf16[768,16]{0,1:T(8,128)(2,1)}, u32[]{:S(2)}) copy-start(bf16[768,16]{0,1:T(8,128)(2,1)} %param.12) | copy-start | bytes 73732
  92.1 4.3 %copy-start.1 = (bf16[2048,1536]{1,0:T(8,128)(2,1)S(1)}, bf16[2048,1536]{1,0:T(8,128)(2,1)}, u32[]{:S(2)}) copy-start(bf16[2048,1536]{1,0:T(8,128)(2,1)} %get-tuple-element.11) | copy-start | bytes 18874372
  96.4 4.4 %copy-start.6 = (s32[4,6,512]{2,1,0:T(8,128)S(1)}, s32[4,6,512]{2,1,0:T(8,128)}, u32[]{:S(2)}) copy-start(s32[4,6,512]{2,1,0:T(8,128)} %get-tuple-element.13) | copy-start | bytes 147460
  96.4 4.4 %copy-start.4 = (bf16[2,768,16]{2,1,0:T(8,128)(2,1)S(1)}, bf16[2,768,16]{2,1,0:T(8,128)(2,1)}, u32[]{:S(2)}) copy-start(bf16[2,768,16]{2,1,0:T(8,128)(2,1)} %get-tuple-element.14) | copy-start | bytes 147460
  108.4 10.2 %slice-start = ((s8[6291456]{0:T(1024)(128)(4,1)}), s8[4194304]{0:T(1024)(128)(4,1)S(1)}, s32[]{:S(2)}) async-start(s8[6291456]{0:T(1024)(128)(4,1)} %bitcast.83), calls=%async_computation | async-start | bytes 8388608
  108.4 10.2 %slice-start.2 = ((s8[6291456]{0:T(1024)(128)(4,1)}), s8[4194304]{0:T(1024)(128)(4,1)S(1)}, s32[]{:S(2)}) async-start(s8[6291456]{0:T(1024)(128)(4,1)} %bitcast.111), calls=%async_computation.2 | async-start | bytes 8388608
  113.3 5.3 %slice-start.1 = ((s8[6291456]{0:T(1024)(128)(4,1)}), s8[2097152]{0:T(1024)(128)(4,1)S(1)}, s32[]{:S(2)}) async-start(s8[6291456]{0:T(1024)(128)(4,1)} %bitcast.83), calls=%async_computation.1 | async-start | bytes 4194304
  113.4 5.3 %slice-start.3 = ((s8[6291456]{0:T(1024)(128)(4,1)}), s8[2097152]{0:T(1024)(128)(4,1)S(1)}, s32[]{:S(2)}) async-start(s8[6291456]{0:T(1024)(128)(4,1)} %bitcast.111), calls=%async_computation.3 | async-start | bytes 4194304
  124.7 2.2 copy-start.3
  134.7 3.2 %copy-start.2 = (bf16[1536,2,512]{2,1,0:T(2,128)(2,1)S(1)}, bf16[1536,2,512]{2,1,0:T(2,128)(2,1)}, u32[]{:S(2)}) copy-start(bf16[1536,2,512]{2,1,0:T(2,128)(2,1)} %param.15) | copy-start | bytes 9437188
  152.9 80.7 %copy-start.9 = (s32[1,4]{1,0:T(1,128)S(1)}, s32[1,4]{1,0:T(1,128)}, u32[]{:S(2)}) copy-start(s32[1,4]{1,0:T(1,128)} %param.19) | copy-start | bytes 52
  152.9 80.9 %copy-start.8 = (s32[1,4]{1,0:T(1,128)S(1)}, s32[1,4]{1,0:T(1,128)}, u32[]{:S(2)}) copy-start(s32[1,4]{1,0:T(1,128)} %param.20) | copy-start | bytes 52
  152.9 81.0 %copy-start.5 = (bf16[256,768]{1,0:T(8,128)(2,1)S(1)}, bf16[256,768]{1,0:T(8,128)(2,1)}, u32[]{:S(2)}) copy-start(bf16[256,768]{1,0:T(8,128)(2,1)} %param.14) | copy-start | bytes 1179652

commit v4 on v3

--- a/solution.py
+++ b/solution.py
@@ -219,10 +219,9 @@
             src_ref=sib.at[k], dst_ref=dst.at[k], send_sem=z_send.at[k], recv_sem=recv.at[k], **dev(r, c)
         )
 
-    order = (3, 0, 2, 1)
-    across = {k: pair(t.at[s, k], sib.at[k], k) for k in order}
-    across[4] = pair(sh.at[s], sh_in, 4)
-    for copy in across.values():
+    order = [k + (z // 2) * (3 - 2 * k) for k in (3, 0, 2, 1)]
+    across = [pair(t.at[s, k], sib.at[k], k) for k in order] + [pair(sh.at[s], sh_in, 4)]
+    for copy in across:
         copy.start()
 
     def add_into(k, other):
@@ -242,10 +241,10 @@
 
         lax.fori_loop(0, 4, one, 0)
 
-    for k in order:
-        across[k].wait_recv()
-
-        if k > 0:
+    for i, k in enumerate(order):
+        across[i].wait_recv()
+
+        if True:
 
             @pl.when((z < k) & (z > 0))
             def _():
@@ -260,7 +259,7 @@
             def _():
                 chain(k, below, up_recv, req + 4).start()
 
-        if k < 3:
+        if True:
 
             @pl.when((z > k) & (z < 3))
             def _():
@@ -304,7 +303,7 @@
         chain(z, above, dn_recv, req - 4).wait_recv()
         more(above)
 
-    for copy in across.values():
+    for copy in across:
         copy.wait_send()
     for k in order:
 

time: 241 us -> 222 us (0.921)
  Pallas kernels: 163 us -> 146 us
    pallas_call x1, Pallas kernels: 80.6 us -> 63.8 us  [give_back(): pl.pallas_call(return_kernel, out_shape=jax.ShapeDtypeStruct(block[1:], j...]
where the time goes in v4:
time: 222 us; the launch traced here: 221 us
  Pallas kernels  146 us (66%)
  matrix products  50.4 us (23%)
  local copies, waits for them, and re-layouts  20.2 us (9%)
  other arithmetic  3.7 us (2%)
    pallas_call x1, Pallas kernels, gather(): pl.pallas_call(gather_kernel, out_shape=(jax.ShapeDtypeStruct((4 * rows,...  82.3 us
    pallas_call x1, Pallas kernels, give_back(): pl.pallas_call(return_kernel, out_shape=jax.ShapeDtypeStruct(block[1:], j...  63.8 us
    dot_general x4, matrix products, body(): up_p = jnp.dot(x_all, gu_all[p, :, half:], preferred_element_type=f32)  15.5 us
    dot_general x4, matrix products, body(): gate_p = jnp.dot(x_all, gu_all[p, :, :half], preferred_element_type=f32)  13 us
    dot_general x2, matrix products, body(): jnp.dot(hidden, down_all[b].reshape(plane * half, feat_local), preferred_...  7.75 us
    another operation x2, local copies, waits for them, and re-layouts, body(): gu = expert_gate_up[0].reshape(feat_local, 2, 2, half).transpose(2, 0, 1, 3)  6.62 us
    slice x1, local copies, waits for them, and re-layouts, body(): shared_gate_up[:, 0, :]  5.9 us
    dot_general x1, matrix products, body(): jnp.dot(shared_hidden, shared_down, preferred_element_type=f32)  4.5 us

profile of v4, /device:TPU:14, one launch (start us, length us, event | category | flops | bytes accessed | tf_op | source)
XLA Modules:
  0.0 220.8 jit_solution(6685284163198292370)
XLA Ops:
  0.0 0.0 copy-start
  0.0 4.0 %reshape_squeeze.12 = bf16[768,2,2,256]{3,2,1,0:T(2,128)(2,1)} reshape(bf16[1,768,1024]{2,1,0:T(8,128)(2,1)} %param.17) | data formatting | bytes 3145728 | tf_op jit(solution)/shard_map/reshape;squeeze | solution.py:365
  4.0 2.6 %copy.35 = bf16[768,2,2,256]{3,1,0,2:T(2,128)(2,1)S(1)} copy(bf16[768,2,2,256]{3,2,1,0:T(2,128)(2,1)} %reshape_squeeze.12) | data formatting | bytes 3145728 | tf_op jit(solution)/shard_map/reshape;squeeze | solution.py:365
  6.6 2.3 %reshape.55.gu = bf16[2,768,512]{2,1,0:T(8,128)(2,1)} reshape(bf16[2,768,2,256]{3,2,1,0:T(2,128)(2,1)S(1)} %bitcast.85) | data formatting | bytes 3145728 | tf_op jit(solution)/shard_map/reshape | solution.py:366
  8.9 0.0 copy-done.7
  8.9 0.8 copy.19.ro
  9.8 82.3 %shard_map.109 = (bf16[2048,1536]{1,0:T(8,128)(2,1)}, bf16[4,2,768,512]{3,2,1,0:T(8,128)(2,1)}, bf16[2,4,256,768]{3,2,1,0:T(8,128)(2,1)}, s32[4,6,512]{2,1,0:T(8...) custom-call(bf16[512,768]{1,0:T(8,128)(2,1)} %x.1, bf16[2,768,512]{2,1,0:T(8,128)(2,1)} %reshape.55.gu, ...), custom_call_target="tpu_custom_call" | custom-call | tf_op jit(solution)/shard_map/pallas_call | solution.py:168
  92.1 0.0 copy-start.1
  92.1 3.4 %fusion.51 = (bf16[1,4,256,768]{3,2,1,0:T(8,128)(2,1)S(1)}, bf16[1,4,256,768]{3,2,1,0:T(8,128)(2,1)}) fusion(bf16[2,4,256,768]{3,2,1,0:T(8,128)(2,1)} %get-tuple-element.15), kind=kLoop, calls=%fused_computation.86 | loop fusion | bytes 6291456 | tf_op jit(solution)/shard_map/slice | solution.py:421
  95.5 0.9 copy-done.1
  96.4 4.4 %fusion.27 = f32[2048,256]{0,1:T(8,128)} fusion(bf16[2048,1536]{1,0:T(8,128)(2,1)S(1)} %copy-done.1, bf16[4,1536,512]{2,1,0:T(8,128)(2,1)} %bitcast.107), kind=kOutput, calls=%fused_computation.43 | convolution fusion | flops 1610612736 | bytes 9175040 | tf_op jit(solution)/shard_map/dot_general | solution.py:416
  100.7 0.0 copy-done.6
  100.8 0.0 copy-done.4
  100.8 1.8 fusion.54
  102.7 5.7 %fusion.7 = bf16[2048,256]{0,1:T(8,128)(2,1)S(1)} fusion(bf16[2048,1536]{1,0:T(8,128)(2,1)} %get-tuple-element.11, f32[2048,256]{0,1:T(8,128)} %fusion.27, f32[2048]{0:T(1024)S(1)} %bitcast.104, bf16[4,1536,512]{2,1,0:T(8,128)(2,1)} %bitcast.108), kind=kOutput, calls=%fused_computation.16 | convolution fusion | flops 1614282752 | bytes 10231808 | tf_op jit(solution)/shard_map/dot_general | solution.py:417
  108.4 0.0 slice-start
  108.4 0.0 slice-start.2
  108.4 4.9 %fusion.28 = f32[2048,256]{0,1:T(8,128)S(1)} fusion(bf16[2048,1536]{1,0:T(8,128)(2,1)} %get-tuple-element.11, bf16[4,1536,512]{2,1,0:T(8,128)(2,1)} %bitcast.109), kind=kOutput, calls=%fused_computation.46 | convolution fusion | flops 1610612736 | bytes 9175040 | tf_op jit(solution)/shard_map/dot_general | solution.py:416
  113.3 0.0 slice-start.1
  113.4 0.0 slice-start.3
  113.4 5.2 %fusion.6 = bf16[2048,256]{0,1:T(8,128)(2,1)S(1)} fusion(bf16[2048,1536]{1,0:T(8,128)(2,1)} %get-tuple-element.11, f32[2048,256]{0,1:T(8,128)S(1)} %fusion.28, f32[2048]{0:T(1024)S(1)} %bitcast.103, bf16[4,1536,512]{2,1,0:T(8,128)(2,1)} %bitcast.110), kind=kOutput, calls=%fused_computation.15 | convolution fusion | flops 1614282752 | bytes 10231808 | tf_op jit(solution)/shard_map/dot_general | solution.py:417
  118.6 0.0 slice-done
  118.6 0.0 slice-done.2
  118.6 0.0 slice-done.1
  118.6 0.0 slice-done.3
  118.7 1.8 fusion.29
  120.5 2.4 %fusion.5 = bf16[2048,256]{0,1:T(8,128)(2,1)S(1)} fusion(bf16[2048,1536]{1,0:T(8,128)(2,1)S(1)} %bitcast.84, f32[2048,256]{0,1:T(8,128)S(1)} %fusion.29, f32[2048]{0:T(1024)S(1)} %bitcast.102, bf16[4,1536,512]{2,1,0:T(8,128)(2,1)S(1)} %bitcast.114), kind=kOutput, calls=%fused_computation.14 | convolution fusion | flops 1614282752 | bytes 10231808 | tf_op jit(solution)/shard_map/dot_general | solution.py:417
  122.9 1.9 fusion.30
  124.7 0.0 copy-start.3
  124.8 2.1 fusion.4
  126.9 0.0 copy-done.3
  126.9 3.9 %convolution_convert_fusion = bf16[2048,768]{1,0:T(8,128)(2,1)S(1)} fusion(bf16[1024,768]{1,0:T(8,128)(2,1)S(1)} %bitcast.89, bf16[2048,256]{0,1:T(8,128)(2,1)S(1)} %fusion.7, bf16[2048,256]{0,1:T(8,128)(2,1)S(1)} %fusion.6, bf16[2048,256]{0,1:T(8,128)(2,1)S(1)} %fusion.5, bf16[2048,256]{0,1:T(8,128)(2,1)S(1)} %fusion.4), kind=kOutput, calls=%fused_computation.2 | convolution fusion | flops 3239575552 | bytes 8912896 | tf_op jit(solution)/shard_map/dot_general | solution.py:421
  130.8 3.9 %convolution_convert_fusion.1 = bf16[2048,768]{1,0:T(8,128)(2,1)S(1)} fusion(bf16[1024,768]{1,0:T(8,128)(2,1)S(1)} %bitcast.88, bf16[2048,256]{0,1:T(8,128)(2,1)S(1)} %fusion.7, bf16[2048,256]{0,1:T(8,128)(2,1)S(1)} %fusion.6, bf16[2048,256]{0,1:T(8,128)(2,1)S(1)} %fusion.5, bf16[2048,256]{0,1:T(8,128)(2,1)S(1)} %fusion.4), kind=kOutput, calls=%fused_computation.3 | convolution fusion | flops 3239575552 | bytes 8912896 | tf_op jit(solution)/shard_map/dot_general | solution.py:421
  134.7 0.0 copy-start.2
  134.7 3.2 %pad_maximum_fusion.t = bf16[2,4,512,768]{3,2,1,0:T(8,128)(2,1)} fusion(bf16[1,4,512,768]{3,2,1,0:T(8,128)(2,1)S(1)} %bitcast.86, bf16[1,4,512,768]{3,2,1,0:T(8,128)(2,1)S(1)} %bitcast.87), kind=kLoop, calls=%fused_computation | loop fusion | flops 3145728 | bytes 12582912 | tf_op jit(solution)/shard_map/stack | solution.py:426
  137.9 5.9 %fusion.50 = (bf16[1536,1,512]{2,1,0:T(2,128)(2,1)}, bf16[1536,1,512]{2,1,0:T(2,128)(2,1)}) fusion(bf16[1536,2,512]{2,1,0:T(2,128)(2,1)S(1)} %copy-done.2), kind=kLoop, calls=%fused_computation.85 | loop fusion | bytes 6291456 | tf_op jit(solution)/shard_map/slice | solution.py:410
  143.8 4.3 %fusion.13 = f32[512,512]{1,0:T(8,128)} fusion(bf16[1536,1,512]{2,1,0:T(2,128)(2,1)} %get-tuple-element.17, bf16[2048,1536]{1,0:T(8,128)(2,1)} %get-tuple-element.11, s32[]{:T(128)S(6)} %select_n.35), kind=kOutput, calls=%fused_computation.26 | convolution fusion | flops 805306368 | bytes 5767172 | tf_op jit(solution)/shard_map/dot_general | solution.py:410
  148.1 4.5 %convolution_convert_fusion.2 = bf16[512,1536]{1,0:T(8,128)(2,1)S(1)} fusion(bf16[512,1536]{1,0:T(8,128)(2,1)S(1)} %copy-done, bf16[1536,1,512]{2,1,0:T(2,128)(2,1)} %get-tuple-element.18, bf16[2048,1536]{1,0:T(8,128)(2,1)} %get-tuple-element.11, s32[]{:T(128)S(6)} %select_n.35, f32[512,512]{1,0:T(8,128)} %fusion.13), kind=kOutput, calls=%fused_computation.4 | convolution fusion | flops 1612972032 | bytes 8912900 | tf_op jit(solution)/shard_map/dot_general | solution.py:413
  152.6 0.1 slice_bitcast_fusion.1
  152.7 0.1 pad_maximum_fusion.2.sh
  152.9 0.0 copy-start.9
  152.9 0.0 copy-start.8
  152.9 0.0 copy-start.5
  152.9 63.8 %shard_map.110 = f32[512,768]{1,0:T(8,128)S(1)} custom-call(bf16[2,4,512,768]{3,2,1,0:T(8,128)(2,1)} %pad_maximum_fusion.t, bf16[2,512,768]{2,1,0:T(8,128)(2,1)S(1)} %pad_maximum_fusion.2.sh), custom_call_target="tpu_custom_call" | custom-call | tf_op jit(solution)/shard_map/pallas_call | solution.py:318
  216.8 0.2 reduce-window.8
  217.0 0.1 convert_reduce_fusion
  217.0 0.1 select_reduce_fusion
  217.1 3.6 %add_convert_fusion = bf16[512,768]{1,0:T(8,128)(2,1)} fusion(f32[512,768]{1,0:T(8,128)S(1)} %shard_map.110, bf16[256,768]{1,0:T(8,128)(2,1)S(1)} %copy-done.5, bf16[1536,256]{1,0:T(8,128)(2,1)} %bitcast.91, bf16[2048,1536]{1,0:T(8,128)(2,1)} %get-tuple-element.11, s32[]{:T(128)S(6)} %select_n.35, s32[256]{0:T(256)S(1)} %and_select_fusion, ...), kind=kOutput, calls=%fused_computation.28 | convolution fusion | flops 605552640 | bytes 5114884 | tf_op jit(solution)/shard_map/dot_general | solution.py:408
  (14 shorter events, 0.1 us)
Async XLA Ops:
  0.0 148.1 %copy-start = (bf16[512,1536]{1,0:T(8,128)(2,1)S(1)}, bf16[512,1536]{1,0:T(8,128)(2,1)}, u32[]{:S(2)}) copy-start(bf16[512,1536]{1,0:T(8,128)(2,1)} %param.16) | copy-start | bytes 4718596
  4.0 5.0 %copy-start.7 = (bf16[768,16]{0,1:T(8,128)(2,1)S(1)}, bf16[768,16]{0,1:T(8,128)(2,1)}, u32[]{:S(2)}) copy-start(bf16[768,16]{0,1:T(8,128)(2,1)} %param.12) | copy-start | bytes 73732
  92.1 4.3 %copy-start.1 = (bf16[2048,1536]{1,0:T(8,128)(2,1)S(1)}, bf16[2048,1536]{1,0:T(8,128)(2,1)}, u32[]{:S(2)}) copy-start(bf16[2048,1536]{1,0:T(8,128)(2,1)} %get-tuple-element.11) | copy-start | bytes 18874372
  96.4 4.4 %copy-start.6 = (s32[4,6,512]{2,1,0:T(8,128)S(1)}, s32[4,6,512]{2,1,0:T(8,128)}, u32[]{:S(2)}) copy-start(s32[4,6,512]{2,1,0:T(8,128)} %get-tuple-element.13) | copy-start | bytes 147460
  96.4 4.4 %copy-start.4 = (bf16[2,768,16]{2,1,0:T(8,128)(2,1)S(1)}, bf16[2,768,16]{2,1,0:T(8,128)(2,1)}, u32[]{:S(2)}) copy-start(bf16[2,768,16]{2,1,0:T(8,128)(2,1)} %get-tuple-element.14) | copy-start | bytes 147460
  108.4 10.2 %slice-start = ((s8[6291456]{0:T(1024)(128)(4,1)}), s8[4194304]{0:T(1024)(128)(4,1)S(1)}, s32[]{:S(2)}) async-start(s8[6291456]{0:T(1024)(128)(4,1)} %bitcast.83), calls=%async_computation | async-start | bytes 8388608
  108.4 10.2 %slice-start.2 = ((s8[6291456]{0:T(1024)(128)(4,1)}), s8[4194304]{0:T(1024)(128)(4,1)S(1)}, s32[]{:S(2)}) async-start(s8[6291456]{0:T(1024)(128)(4,1)} %bitcast.111), calls=%async_computation.2 | async-start | bytes 8388608
  113.3 5.3 %slice-start.1 = ((s8[6291456]{0:T(1024)(128)(4,1)}), s8[2097152]{0:T(1024)(128)(4,1)S(1)}, s32[]{:S(2)}) async-start(s8[6291456]{0:T(1024)(128)(4,1)} %bitcast.83), calls=%async_computation.1 | async-start | bytes 4194304
  113.4 5.3 %slice-start.3 = ((s8[6291456]{0:T(1024)(128)(4,1)}), s8[2097152]{0:T(1024)(128)(4,1)S(1)}, s32[]{:S(2)}) async-start(s8[6291456]{0:T(1024)(128)(4,1)} %bitcast.111), calls=%async_computation.3 | async-start | bytes 4194304
  124.7 2.2 copy-start.3
  134.7 3.2 %copy-start.2 = (bf16[1536,2,512]{2,1,0:T(2,128)(2,1)S(1)}, bf16[1536,2,512]{2,1,0:T(2,128)(2,1)}, u32[]{:S(2)}) copy-start(bf16[1536,2,512]{2,1,0:T(2,128)(2,1)} %param.15) | copy-start | bytes 9437188
  152.9 63.9 %copy-start.9 = (s32[1,4]{1,0:T(1,128)S(1)}, s32[1,4]{1,0:T(1,128)}, u32[]{:S(2)}) copy-start(s32[1,4]{1,0:T(1,128)} %param.19) | copy-start | bytes 52
  152.9 64.2 %copy-start.8 = (s32[1,4]{1,0:T(1,128)S(1)}, s32[1,4]{1,0:T(1,128)}, u32[]{:S(2)}) copy-start(s32[1,4]{1,0:T(1,128)} %param.20) | copy-start | bytes 52
  152.9 64.2 %copy-start.5 = (bf16[256,768]{1,0:T(8,128)(2,1)S(1)}, bf16[256,768]{1,0:T(8,128)(2,1)}, u32[]{:S(2)}) copy-start(bf16[256,768]{1,0:T(8,128)(2,1)} %param.14) | copy-start | bytes 1179652
